TPU v7x, 512 devices: a whole 4x8x8 slice. The times are simulated.
512 devices in a mesh: ex: 16 (over y_lo, z), feat: 32 (over x, y_hi, core).
Axes of the slice: x: 4, y: 8 (y_hi: 4, y_lo: 2; y = y_hi * 2 + y_lo), z: 8, core: 2. Of those that a mesh axis runs over, the one named last changes fastest.
Arguments:
- grads: float32 [4096, 8192], P('ex', 'feat'), may hold values from -6 to 6
- second_moment: float32 [8192], P('feat'), may hold values from 0.0001 to 0.01
Outputs:
- similarity: float32 [4096, 4096], P(('ex', 'feat'))
All inputs are finite; a program needn't handle non-finite values.
Results may differ from a plain program's by a relative error of at most 0.000096.
Values sent between devices are 32-bit elements; how exact they have to be, the bound alone decides.
No kernel may reach another device: no remote copies, remote signals or barrier semaphores. Data moves between devices by JAX's collectives and lax.ppermute only.
A program may use at most 64 MiB of HBM per device.

v0:
```python
import jax
import jax.numpy as jnp
import numpy as np
from jax import lax
from jax.sharding import PartitionSpec as P


def pair_tables(blocks_n):
    first_of = []
    second_of = []
    for first in range(blocks_n):
        for second in range(first, blocks_n):
            first_of.append(first)
            second_of.append(second)
    count = len(first_of)
    width = (count + blocks_n - 1) // blocks_n
    mine = np.zeros((blocks_n, width), np.int32)
    where = np.zeros((blocks_n, blocks_n), np.int32)
    filled = np.zeros(blocks_n, np.int32)
    for tile in range(count):
        owner = tile % blocks_n
        slot = filled[owner]
        mine[owner, slot] = tile
        filled[owner] = slot + 1
        first = first_of[tile]
        second = second_of[tile]
        where[first, second] = (owner * width + slot) * 2
        where[second, first] = (owner * width + slot) * 2 + 1
    return (np.array(first_of, np.int32), np.array(second_of, np.int32), mine, where)


def shards(grads, second_moment):
    scaled = grads / (jnp.sqrt(second_moment) + 1e-08)[None, :]
    row_sq = lax.psum(jnp.sum(scaled * scaled, axis=1), "feat")
    unit = scaled / jnp.sqrt(row_sq + 1e-06)[:, None]
    block_rows = unit.shape[0]
    blocks_n = lax.axis_size("ex")
    every = lax.all_gather(unit, "ex", axis=0, tiled=True)
    first_of, second_of, mine, where = pair_tables(blocks_n)
    index_ex = lax.axis_index("ex")
    my_tiles = jnp.take(jnp.asarray(mine), index_ex, axis=0)
    stacked = every.reshape(blocks_n, block_rows, every.shape[1])
    left = jnp.take(stacked, jnp.take(jnp.asarray(first_of), my_tiles), axis=0)
    right = jnp.take(stacked, jnp.take(jnp.asarray(second_of), my_tiles), axis=0)
    partial_tiles = jnp.einsum(
        "krd,ksd->krs",
        left,
        right,
        precision=lax.Precision.HIGHEST,
        preferred_element_type=jnp.float32,
    )
    summed = lax.psum_scatter(partial_tiles, "feat", scatter_dimension=1, tiled=True)
    turned = lax.all_to_all(summed, "feat", split_axis=2, concat_axis=1, tiled=True)
    both_ways = jnp.stack([summed, jnp.swapaxes(turned, 1, 2)], axis=1)
    arrived = lax.all_gather(both_ways, "ex", axis=0, tiled=True)
    slice_rows = summed.shape[1]
    flat = arrived.reshape(-1, slice_rows, block_rows)
    picks = jnp.take(jnp.asarray(where), index_ex, axis=0)
    chosen = jnp.take(flat, picks, axis=0)
    return jnp.transpose(chosen, (1, 0, 2)).reshape(slice_rows, blocks_n * block_rows)


def solution(mesh):
    return jax.shard_map(
        shards,
        mesh=mesh,
        in_specs=(P("ex", "feat"), P("feat")),
        out_specs=P(("ex", "feat"), None),
        check_vma=False,
    )
```

profile of v0, /device:TPU:6, one launch (start us, length us, event | category | flops | bytes accessed | tf_op | source)
XLA Modules:
  0.0 378.8 jit_solution(9070327241805598290)
XLA Ops:
  6.5 0.7 sqrt_add_fusion
  7.2 1.1 multiply_reduce_fusion
  8.3 64.1 %psum.7 = f32[256]{0:T(256)S(1)} all-reduce(f32[256]{0:T(256)S(1)} %multiply_reduce_fusion), channel_id=1, replica_groups=mesh['ex'=16,'feat'=32] {'feat'}, use_global_device_ids=true, to_apply=%region_1.0 | all-reduce | flops 256 | bytes 2048 | tf_op jit(solution)/shard_map/psum | solution.py:34
  72.4 1.8 multiply_divide_fusion
  74.3 0.7 compare_select_fusion.2
  75.0 1.3 gather_fusion.1
  76.3 1.3 gather_fusion.3
  77.7 0.7 compare_and_fusion.1
  78.4 85.0 %all-gather.3.cloned.1.call-done = f32[4096,256]{1,0:T(8,128)} async-done(((f32[256,256]{1,0:T(8,128)}), f32[4096,256]{1,0:T(8,128)}) %all-gather.3.cloned.1.call-update) | async-done | bytes 4194320 | tf_op jit(solution)/shard_map/all_gather | solution.py:38
  163.3 2.9 gather_fusion.2
  166.2 4.3 %gather_fusion.4 = f32[9,256,256]{2,1,0:T(8,128)} fusion(f32[16,256,256]{2,1,0:T(8,128)} %bitcast.32, s32[1024]{0:T(1024)S(1)} %get-tuple-element.53), kind=kCustom, calls=%fused_computation.3.clone | custom fusion | bytes 4718628 | tf_op jit(solution)/shard_map/jit(_take)/gather | solution.py:44
  170.6 5.6 %fusion = f32[9,256,256]{2,1,0:T(8,128)} fusion(f32[9,256,256]{2,1,0:T(8,128)} %gather_fusion.4, f32[9,256,256]{2,1,0:T(8,128)S(1)} %gather_fusion.2, pred[9]{0:T(512)(128)(4,1)S(1)} %get-tuple-element.51, pred[9]{0:T(512)(128)(4,1)S(1)} %get-tuple-element.47), kind=kOutput, calls=%fused_computation.5 | convolution fusion | flops 1813118976 | bytes 7077906 | tf_op jit(solution)/shard_map/krd,ksd->krs/dot_general | solution.py:45
  176.2 97.2 %reduce-scatter.2.cloned.1.call-done = f32[9,8,256]{2,1,0:T(8,128)} async-done(((f32[9,256,256]{2,1,0:T(8,128)}), f32[9,8,256]{2,1,0:T(8,128)}) %reduce-scatter.2.cloned.1.call-update) | async-done | bytes 73744 | tf_op jit(solution)/shard_map/reduce_scatter | solution.py:52
  273.4 1.3 copy.14
  274.7 0.8 reshape.162
  275.6 15.5 %all_to_all.18 = f32[32,1,576]{2,1,0:T(1,128)S(1)} all-to-all(f32[32,1,576]{2,1,0:T(1,128)S(1)} %reshape.162), channel_id=1, replica_groups=mesh['ex'=16,'feat'=32] {'feat'}, dimensions={0} | all-to-all | bytes 147456 | tf_op jit(solution)/shard_map/all_to_all | solution.py:53
  291.5 0.9 reduce
  292.4 1.1 reshape.163
  293.5 1.7 copy.16
  296.4 0.7 fusion.7
  297.1 0.7 compare_and_fusion.3
  297.8 71.1 %all-gather.5.cloned.1.call-done = f32[144,2,8,256]{3,2,0,1:T(8,128)} async-done(((f32[9,2,8,256]{3,2,0,1:T(8,128)}), f32[144,2,8,256]{3,2,0,1:T(8,128)}) %all-gather.5.cloned.1.call-update) | async-done | bytes 2359312 | tf_op jit(solution)/shard_map/all_gather | solution.py:55
  368.9 2.0 copy.17
  371.5 0.7 broadcast_select_fusion
  (16 shorter events, 2.5 us)
Async XLA Ops:
  6.5 156.8 %all-gather.3.cloned.1.call-start = ((), (), s32[]{:S(2)}) async-start(), calls=%async_computation.2 | async-start | bytes 4456448 | tf_op jit(solution)/shard_map/all_gather | solution.py:38
  74.2 199.2 %reduce-scatter.2.cloned.1.call-start = ((), (), s32[]{:S(2)}) async-start(), calls=%async_computation.3 | async-start | bytes 2433024 | tf_op jit(solution)/shard_map/reduce_scatter | solution.py:52
  176.2 192.8 %all-gather.5.cloned.1.call-start = ((), (), s32[]{:S(2)}) async-start(), calls=%async_computation.4 | async-start | bytes 2506752 | tf_op jit(solution)/shard_map/all_gather | solution.py:55
  291.5 4.2 %copy-start = (f32[9,8,256]{2,1,0:T(8,128)S(1)}, f32[9,8,256]{2,1,0:T(8,128)}, u32[]{:S(2)}) copy-start(f32[9,8,256]{2,1,0:T(8,128)} %reduce-scatter.2.cloned.1.call-done) | copy-start | bytes 221188
Sparse Core Ops, SparseCore 0:
  74.3 88.9 all-gather.2
  176.3 97.0 reduce-scatter.1
  296.6 72.3 all-gather.4
where the time goes:
time: 379 us
  waiting for transfers between devices  253 us (67%)
  blocking collectives  79.6 us (21%)
  local copies, waits for them, and re-layouts  18.5 us (5%)
  between operations  13.2 us (3%)
  other arithmetic  8.61 us (2%)
  matrix products  5.59 us (1%)
    reduce_scatter x1, waiting for transfers between devices, shards(): lax.psum_scatter(partial_tiles, 'feat', scatter_dimension=1, tiled=True)  97.2 us
    all_gather x1, waiting for transfers between devices, shards(): every = lax.all_gather(unit, 'ex', axis=0, tiled=True)  85 us
    all_gather x1, waiting for transfers between devices, shards(): arrived = lax.all_gather(both_ways, 'ex', axis=0, tiled=True)  71.1 us
    psum x1, blocking collectives, shards(): row_sq = lax.psum(jnp.sum(scaled * scaled, axis=1), 'feat')  64.1 us
    all_to_all x1, blocking collectives, shards(): lax.all_to_all(summed, 'feat', split_axis=2, concat_axis=1, tiled=True)  15.5 us
  transfers between devices with their start and end apart: 3, of which 3 were waited for; matrix products, arithmetic and copies ran while one was open for 1% of the time, Pallas kernels for 0%

commit v1 on v0

v1 whole, which is shorter than its diff:
```python
import jax
import jax.numpy as jnp
from jax import lax
from jax.sharding import PartitionSpec as P

XS, YH, YL, ZS, CS = 4, 4, 2, 8, 2
YS = YH * YL
FEAT = XS * YH * CS
AXES = ("ex", "feat")


def device_at(x, y, z, c):
    return ((y % YL) * ZS + z) * FEAT + x * (YH * CS) + (y // YL) * CS + c


YH_GROUPS = [[x * (YH * CS) + yh * CS + c for yh in range(YH)] for x in range(XS) for c in range(CS)]
XY_GROUPS = [[device_at(x, y, z, c) for x in range(XS) for y in range(YS)]
             for z in range(ZS) for c in range(CS)]


def shift(value, move):
    pairs = []
    for x in range(XS):
        for y in range(YS):
            for z in range(ZS):
                for c in range(CS):
                    nx, ny, nz, nc = move(x, y, z, c)
                    pairs.append((device_at(x, y, z, c), device_at(nx % XS, ny % YS, nz % ZS, nc % CS)))
    return lax.ppermute(value, AXES, pairs)


def rings(piece):
    along_y = {0: piece}
    along_z = {0: piece}
    for step in range(1, 5):
        for way in (1, -1):
            if step == 4 and way < 0:
                continue
            at, before = way * step, way * (step - 1)
            turn = lambda c: -way if c == 0 else way
            along_y[at] = shift(along_y[before], lambda x, y, z, c: (x, y + turn(c), z, c))
            along_z[at] = shift(along_z[before], lambda x, y, z, c: (x, y, z + turn(c), c))
    return along_y, along_z


def placed(along_y, along_z, y, z, sign):
    whole = jnp.zeros((16,) + along_y[0].shape, jnp.float32)
    for t in along_y:
        whole = lax.dynamic_update_slice(whole, along_y[t][None], ((y + sign * t) % 8, 0, 0))
        whole = lax.dynamic_update_slice(whole, along_z[t][None], (8 + (z + sign * t) % 8, 0, 0))
    whole = whole.reshape(2, 512, -1)
    return whole[0], whole[1]


def shards(grads, second_moment):
    ex, feat = lax.axis_index("ex"), lax.axis_index("feat")
    z, y_lo = ex % ZS, ex // ZS
    y_hi, core = (feat // CS) % YH, feat % CS
    y = y_hi * YL + y_lo
    sign = 1 - 2 * core

    scaled = grads * (1.0 / (jnp.sqrt(second_moment) + 1e-08))[None, :]
    swapped = lax.all_to_all(scaled.reshape(YH, 64, 256), "feat", 0, 0, axis_index_groups=YH_GROUPS, tiled=True)
    piece = jnp.transpose(swapped, (1, 0, 2)).reshape(64, YH * 256)
    along_y, along_z = rings(piece)
    left, right = placed(along_y, along_z, y, z, sign)

    part = lax.dot_general(left, right, (((1,), (1,)), ((), ())), precision=lax.Precision.HIGH,
                           preferred_element_type=jnp.float32)
    sq = jnp.sum(right * right, axis=1)

    part = jnp.transpose(part.reshape(XS, YL, YH, CS, 8, 4, 128), (3, 0, 2, 1, 5, 4, 6)).reshape(CS, XS * YS, 4, 8, 128)
    sq = jnp.broadcast_to(jnp.pad(sq.reshape(4, 128), ((0, 4), (0, 0))), (CS, XS * YS, 1, 8, 128))
    part = jnp.concatenate([part, sq], axis=2)
    take = lambda i: lax.dynamic_index_in_dim(part, i, 0, keepdims=False)
    part = take(core) + shift(take(1 - core), lambda x, y, z, c: (x, y, z, c + 1))
    whole = lax.all_to_all(part, AXES, 0, 0, axis_index_groups=XY_GROUPS, tiled=True)
    whole = jnp.sum(whole.reshape(XS, YS, 5, 8, 128), axis=0)

    scale = lax.rsqrt(whole[:, 4, :4] + 1e-06)
    scale = jnp.transpose(scale.reshape(YH, YL, ZS, 64), (1, 2, 0, 3)).reshape(4096)
    out = whole[:, :4].reshape(YH, YL, 4, 8, 2, 64)
    out = jnp.transpose(out, (3, 1, 2, 4, 0, 5)).reshape(8, 4096)
    own = lax.dynamic_slice(scale, (ex * 256 + feat * 8,), (8,))
    return out * scale[None, :] * own[:, None]


def solution(mesh):
    return jax.shard_map(
        shards,
        mesh=mesh,
        in_specs=(P("ex", "feat"), P("feat")),
        out_specs=P(("ex", "feat"), None),
        check_vma=False,
    )
```

time: 379 us -> 119 us (0.31)
  the two profiles are of different devices: /device:TPU:6 before, /device:TPU:8 now
where the time goes in v1:
time: 119 us
  starting transfers between devices  66.6 us (56%)
  waiting for transfers between devices  26.4 us (22%)
  blocking collectives  16.8 us (14%)
  other arithmetic  3.88 us (3%)
  local copies, waits for them, and re-layouts  2.28 us (2%)
  matrix products  1.85 us (2%)
    ppermute x15, starting transfers between devices, shift(): return lax.ppermute(value, AXES, pairs)  55.2 us
    all_to_all x1, waiting for transfers between devices, shards(): lax.all_to_all(part, AXES, 0, 0, axis_index_groups=XY_GROUPS, tiled=True)  20.6 us
    all_to_all x1, blocking collectives, shards(): lax.all_to_all(scaled.reshape(YH, 64, 256), 'feat', 0, 0, axis_index_grou...  16.8 us
    all_to_all x1, starting transfers between devices, shards(): lax.all_to_all(part, AXES, 0, 0, axis_index_groups=XY_GROUPS, tiled=True)  11.4 us
    ppermute x15, waiting for transfers between devices, shift(): return lax.ppermute(value, AXES, pairs)  5.78 us
  transfers between devices with their start and end apart: 16, of which 4 were waited for; matrix products, arithmetic and copies ran while one was open for 1% of the time, Pallas kernels for 0%

profile of v1, /device:TPU:8, one launch (start us, length us, event | category | flops | bytes accessed | tf_op | source)
XLA Modules:
  0.0 118.7 jit_solution(580821173084857214)
XLA Ops:
  0.7 1.0 broadcast_multiply_fusion
  1.7 16.8 %all_to_all.10 = f32[4,64,256]{2,1,0:T(8,128)S(1)} all-to-all(f32[4,64,256]{2,1,0:T(8,128)S(1)} %bitcast.65), channel_id=1, replica_groups={{0,2,4,6},{1,3,5,7},{8,10,12,14},{9,11,13,15},{16,18,20,22},{17,19,21,2..., dimensions={0} | all-to-all | bytes 524288 | tf_op jit(solution)/shard_map/all_to_all | solution.py:63
  18.5 3.2 %collective-permute-start = (f32[64,1024]{1,0:T(8,128)S(1)}, f32[64,1024]{1,0:T(8,128)S(1)}, u32[]{:S(2)}, u32[]{:S(2)}) collective-permute-start(f32[64,1024]{1,0:T(8,128)S(1)} %bitcast.67), channel_id=1, source_target_pairs={{0,262},{1,257},{32,294},{33,289},{64,326},{65,321},{96,358},{97,3... | collective-permute-start | bytes 786440 | tf_op jit(solution)/shard_map/ppermute | solution.py:29
  21.8 10.9 %collective-permute-start.1 = (f32[64,1024]{1,0:T(8,128)S(1)}, f32[64,1024]{1,0:T(8,128)S(1)}, u32[]{:S(2)}, u32[]{:S(2)}) collective-permute-start(f32[64,1024]{1,0:T(8,128)S(1)} %bitcast.68), channel_id=1, source_target_pairs={{0,224},{1,33},{32,0},{33,65},{64,32},{65,97},{96,64},{97,129},{12... | collective-permute-start | bytes 786440 | tf_op jit(solution)/shard_map/ppermute | solution.py:29
  32.7 2.6 %collective-permute-start.2 = (f32[64,1024]{1,0:T(8,128)S(1)}, f32[64,1024]{1,0:T(8,128)S(1)}, u32[]{:S(2)}, u32[]{:S(2)}) collective-permute-start(f32[64,1024]{1,0:T(8,128)S(1)} %bitcast.69), channel_id=1, source_target_pairs={{0,256},{1,263},{32,288},{33,295},{64,320},{65,327},{96,352},{97,3... | collective-permute-start | bytes 786440 | tf_op jit(solution)/shard_map/ppermute | solution.py:29
  35.4 1.9 %collective-permute-start.3 = (f32[64,1024]{1,0:T(8,128)S(1)}, f32[64,1024]{1,0:T(8,128)S(1)}, u32[]{:S(2)}, u32[]{:S(2)}) collective-permute-start(f32[64,1024]{1,0:T(8,128)S(1)} %bitcast.70), channel_id=1, source_target_pairs={{0,32},{1,225},{32,64},{33,1},{64,96},{65,33},{96,128},{97,65},{12... | collective-permute-start | bytes 786440 | tf_op jit(solution)/shard_map/ppermute | solution.py:29
  38.5 3.2 %collective-permute-start.4 = (f32[64,1024]{1,0:T(8,128)S(1)}, f32[64,1024]{1,0:T(8,128)S(1)}, u32[]{:S(2)}, u32[]{:S(2)}) collective-permute-start(f32[64,1024]{1,0:T(8,128)S(1)} %collective-permute-done), channel_id=1, source_target_pairs={{0,262},{1,257},{32,294},{33,289},{64,326},{65,321},{96,358},{97,3... | collective-permute-start | bytes 786440 | tf_op jit(solution)/shard_map/ppermute | solution.py:29
  41.8 5.1 %collective-permute-start.5 = (f32[64,1024]{1,0:T(8,128)S(1)}, f32[64,1024]{1,0:T(8,128)S(1)}, u32[]{:S(2)}, u32[]{:S(2)}) collective-permute-start(f32[64,1024]{1,0:T(8,128)S(1)} %collective-permute-done.1), channel_id=1, source_target_pairs={{0,224},{1,33},{32,0},{33,65},{64,32},{65,97},{96,64},{97,129},{12... | collective-permute-start | bytes 786440 | tf_op jit(solution)/shard_map/ppermute | solution.py:29
  46.9 2.6 %collective-permute-start.6 = (f32[64,1024]{1,0:T(8,128)S(1)}, f32[64,1024]{1,0:T(8,128)S(1)}, u32[]{:S(2)}, u32[]{:S(2)}) collective-permute-start(f32[64,1024]{1,0:T(8,128)S(1)} %collective-permute-done.2), channel_id=1, source_target_pairs={{0,256},{1,263},{32,288},{33,295},{64,320},{65,327},{96,352},{97,3... | collective-permute-start | bytes 786440 | tf_op jit(solution)/shard_map/ppermute | solution.py:29
  49.6 1.9 %collective-permute-start.7 = (f32[64,1024]{1,0:T(8,128)S(1)}, f32[64,1024]{1,0:T(8,128)S(1)}, u32[]{:S(2)}, u32[]{:S(2)}) collective-permute-start(f32[64,1024]{1,0:T(8,128)S(1)} %collective-permute-done.3), channel_id=1, source_target_pairs={{0,32},{1,225},{32,64},{33,1},{64,96},{65,33},{96,128},{97,65},{12... | collective-permute-start | bytes 786440 | tf_op jit(solution)/shard_map/ppermute | solution.py:29
  51.6 3.2 %collective-permute-start.8 = (f32[64,1024]{1,0:T(8,128)S(1)}, f32[64,1024]{1,0:T(8,128)S(1)}, u32[]{:S(2)}, u32[]{:S(2)}) collective-permute-start(f32[64,1024]{1,0:T(8,128)S(1)} %collective-permute-done.4), channel_id=1, source_target_pairs={{0,262},{1,257},{32,294},{33,289},{64,326},{65,321},{96,358},{97,3... | collective-permute-start | bytes 786440 | tf_op jit(solution)/shard_map/ppermute | solution.py:29
  54.9 5.1 %collective-permute-start.9 = (f32[64,1024]{1,0:T(8,128)S(1)}, f32[64,1024]{1,0:T(8,128)S(1)}, u32[]{:S(2)}, u32[]{:S(2)}) collective-permute-start(f32[64,1024]{1,0:T(8,128)S(1)} %collective-permute-done.5), channel_id=1, source_target_pairs={{0,224},{1,33},{32,0},{33,65},{64,32},{65,97},{96,64},{97,129},{12... | collective-permute-start | bytes 786440 | tf_op jit(solution)/shard_map/ppermute | solution.py:29
  60.0 2.6 %collective-permute-start.10 = (f32[64,1024]{1,0:T(8,128)S(1)}, f32[64,1024]{1,0:T(8,128)S(1)}, u32[]{:S(2)}, u32[]{:S(2)}) collective-permute-start(f32[64,1024]{1,0:T(8,128)S(1)} %collective-permute-done.6), channel_id=1, source_target_pairs={{0,256},{1,263},{32,288},{33,295},{64,320},{65,327},{96,352},{97,3... | collective-permute-start | bytes 786440 | tf_op jit(solution)/shard_map/ppermute | solution.py:29
  62.7 1.9 %collective-permute-start.11 = (f32[64,1024]{1,0:T(8,128)S(1)}, f32[64,1024]{1,0:T(8,128)S(1)}, u32[]{:S(2)}, u32[]{:S(2)}) collective-permute-start(f32[64,1024]{1,0:T(8,128)S(1)} %collective-permute-done.7), channel_id=1, source_target_pairs={{0,32},{1,225},{32,64},{33,1},{64,96},{65,33},{96,128},{97,65},{12... | collective-permute-start | bytes 786440 | tf_op jit(solution)/shard_map/ppermute | solution.py:29
  64.7 3.7 %collective-permute-start.12 = (f32[64,1024]{1,0:T(8,128)S(1)}, f32[64,1024]{1,0:T(8,128)S(1)}, u32[]{:S(2)}, u32[]{:S(2)}) collective-permute-start(f32[64,1024]{1,0:T(8,128)S(1)} %collective-permute-done.8), channel_id=1, source_target_pairs={{0,262},{1,257},{32,294},{33,289},{64,326},{65,321},{96,358},{97,3... | collective-permute-start | bytes 786440 | tf_op jit(solution)/shard_map/ppermute | solution.py:29
  68.4 5.1 %collective-permute-start.13 = (f32[64,1024]{1,0:T(8,128)S(1)}, f32[64,1024]{1,0:T(8,128)S(1)}, u32[]{:S(2)}, u32[]{:S(2)}) collective-permute-start(f32[64,1024]{1,0:T(8,128)S(1)} %collective-permute-done.9), channel_id=1, source_target_pairs={{0,224},{1,33},{32,0},{33,65},{64,32},{65,97},{96,64},{97,129},{12... | collective-permute-start | bytes 786440 | tf_op jit(solution)/shard_map/ppermute | solution.py:29
  74.2 3.2 %collective-permute-done.13 = f32[64,1024]{1,0:T(8,128)S(1)} collective-permute-done((f32[64,1024]{1,0:T(8,128)S(1)}, f32[64,1024]{1,0:T(8,128)S(1)}, u32[]{:S(2)}, u32[]{:S(2)}) %collective-permute-start.13) | collective-permute-done | bytes 262176 | tf_op jit(solution)/shard_map/ppermute | solution.py:29
  77.9 1.9 %convolution_bitcast_fusion = f32[2,4,4,2,4,8,128]{6,5,4,0,2,3,1:T(8,128)S(1)} fusion(f32[4,2,4,2,8,1024,1]{5,4,6,3,2,1,0:T(8,128)S(1)} %bitcast.61, f32[4,128,1024,1,1,1,1]{2,1,0,6,5,4,3:T(8,128)S(1)} %bitcast.60), kind=kOutput, calls=%fused_computation.3 | convolution fusion | flops 1610612736 | bytes 5242880 | tf_op jit(solution)/shard_map/dot_general | solution.py:68
  80.1 1.9 %collective-permute-start.14 = (f32[32,5,8,128]{3,2,1,0:T(8,128)S(1)}, f32[32,5,8,128]{3,2,1,0:T(8,128)S(1)}, u32[]{:S(2)}, u32[]{:S(2)}) collective-permute-start(f32[32,5,8,128]{3,2,1,0:T(8,128)S(1)} %fusion.1), channel_id=1, source_target_pairs={{0,1},{1,0},{32,33},{33,32},{64,65},{65,64},{96,97},{97,96},{128,1... | collective-permute-start | bytes 1966088 | tf_op jit(solution)/shard_map/ppermute | solution.py:29
  82.0 2.1 %collective-permute-done.14 = f32[32,5,8,128]{3,2,1,0:T(8,128)S(1)} collective-permute-done((f32[32,5,8,128]{3,2,1,0:T(8,128)S(1)}, f32[32,5,8,128]{3,2,1,0:T(8,128)S(1)}, u32[]{:S(2)}, u32[]{:S(2)}) %collective-permute-start.14) | collective-permute-done | bytes 655392 | tf_op jit(solution)/shard_map/ppermute | solution.py:29
  84.1 0.9 fusion.4
  85.0 11.4 %all-to-all-start.1 = ((f32[32,5,8,128]{3,2,1,0:T(8,128)}), f32[32,5,8,128]{3,2,1,0:T(8,128)S(1)}, u32[]{:S(2)}, u32[]{:S(2)}) async-start(f32[32,5,8,128]{3,2,1,0:T(8,128)} %fusion.4), calls=%async_computation.1 | async-start | bytes 1310720 | tf_op jit(solution)/shard_map/all_to_all | solution.py:77
  96.4 20.6 %all-to-all-done.1 = f32[32,5,8,128]{3,2,1,0:T(8,128)S(1)} async-done(((f32[32,5,8,128]{3,2,1,0:T(8,128)}), f32[32,5,8,128]{3,2,1,0:T(8,128)S(1)}, u32[]{:S(2)}, u32[]{:S(2)}) %all-to-all-start.1) | async-done | bytes 655392 | tf_op jit(solution)/shard_map/all_to_all | solution.py:77
  117.9 0.7 multiply_multiply_fusion
  (50 shorter events, 4.1 us)
Async XLA Ops:
  18.5 20.0 %collective-permute-start = (f32[64,1024]{1,0:T(8,128)S(1)}, f32[64,1024]{1,0:T(8,128)S(1)}, u32[]{:S(2)}, u32[]{:S(2)}) collective-permute-start(f32[64,1024]{1,0:T(8,128)S(1)} %bitcast.67), channel_id=1, source_target_pairs={{0,262},{1,257},{32,294},{33,289},{64,326},{65,321},{96,358},{97,3... | collective-permute-start | bytes 786440 | tf_op jit(solution)/shard_map/ppermute | solution.py:29
  21.8 20.0 %collective-permute-start.1 = (f32[64,1024]{1,0:T(8,128)S(1)}, f32[64,1024]{1,0:T(8,128)S(1)}, u32[]{:S(2)}, u32[]{:S(2)}) collective-permute-start(f32[64,1024]{1,0:T(8,128)S(1)} %bitcast.68), channel_id=1, source_target_pairs={{0,224},{1,33},{32,0},{33,65},{64,32},{65,97},{96,64},{97,129},{12... | collective-permute-start | bytes 786440 | tf_op jit(solution)/shard_map/ppermute | solution.py:29
  32.7 14.2 %collective-permute-start.2 = (f32[64,1024]{1,0:T(8,128)S(1)}, f32[64,1024]{1,0:T(8,128)S(1)}, u32[]{:S(2)}, u32[]{:S(2)}) collective-permute-start(f32[64,1024]{1,0:T(8,128)S(1)} %bitcast.69), channel_id=1, source_target_pairs={{0,256},{1,263},{32,288},{33,295},{64,320},{65,327},{96,352},{97,3... | collective-permute-start | bytes 786440 | tf_op jit(solution)/shard_map/ppermute | solution.py:29
  35.4 14.2 %collective-permute-start.3 = (f32[64,1024]{1,0:T(8,128)S(1)}, f32[64,1024]{1,0:T(8,128)S(1)}, u32[]{:S(2)}, u32[]{:S(2)}) collective-permute-start(f32[64,1024]{1,0:T(8,128)S(1)} %bitcast.70), channel_id=1, source_target_pairs={{0,32},{1,225},{32,64},{33,1},{64,96},{65,33},{96,128},{97,65},{12... | collective-permute-start | bytes 786440 | tf_op jit(solution)/shard_map/ppermute | solution.py:29
  38.5 13.1 %collective-permute-start.4 = (f32[64,1024]{1,0:T(8,128)S(1)}, f32[64,1024]{1,0:T(8,128)S(1)}, u32[]{:S(2)}, u32[]{:S(2)}) collective-permute-start(f32[64,1024]{1,0:T(8,128)S(1)} %collective-permute-done), channel_id=1, source_target_pairs={{0,262},{1,257},{32,294},{33,289},{64,326},{65,321},{96,358},{97,3... | collective-permute-start | bytes 786440 | tf_op jit(solution)/shard_map/ppermute | solution.py:29
  41.8 13.1 %collective-permute-start.5 = (f32[64,1024]{1,0:T(8,128)S(1)}, f32[64,1024]{1,0:T(8,128)S(1)}, u32[]{:S(2)}, u32[]{:S(2)}) collective-permute-start(f32[64,1024]{1,0:T(8,128)S(1)} %collective-permute-done.1), channel_id=1, source_target_pairs={{0,224},{1,33},{32,0},{33,65},{64,32},{65,97},{96,64},{97,129},{12... | collective-permute-start | bytes 786440 | tf_op jit(solution)/shard_map/ppermute | solution.py:29
  46.9 13.1 %collective-permute-start.6 = (f32[64,1024]{1,0:T(8,128)S(1)}, f32[64,1024]{1,0:T(8,128)S(1)}, u32[]{:S(2)}, u32[]{:S(2)}) collective-permute-start(f32[64,1024]{1,0:T(8,128)S(1)} %collective-permute-done.2), channel_id=1, source_target_pairs={{0,256},{1,263},{32,288},{33,295},{64,320},{65,327},{96,352},{97,3... | collective-permute-start | bytes 786440 | tf_op jit(solution)/shard_map/ppermute | solution.py:29
  49.6 13.1 %collective-permute-start.7 = (f32[64,1024]{1,0:T(8,128)S(1)}, f32[64,1024]{1,0:T(8,128)S(1)}, u32[]{:S(2)}, u32[]{:S(2)}) collective-permute-start(f32[64,1024]{1,0:T(8,128)S(1)} %collective-permute-done.3), channel_id=1, source_target_pairs={{0,32},{1,225},{32,64},{33,1},{64,96},{65,33},{96,128},{97,65},{12... | collective-permute-start | bytes 786440 | tf_op jit(solution)/shard_map/ppermute | solution.py:29
  51.6 13.1 %collective-permute-start.8 = (f32[64,1024]{1,0:T(8,128)S(1)}, f32[64,1024]{1,0:T(8,128)S(1)}, u32[]{:S(2)}, u32[]{:S(2)}) collective-permute-start(f32[64,1024]{1,0:T(8,128)S(1)} %collective-permute-done.4), channel_id=1, source_target_pairs={{0,262},{1,257},{32,294},{33,289},{64,326},{65,321},{96,358},{97,3... | collective-permute-start | bytes 786440 | tf_op jit(solution)/shard_map/ppermute | solution.py:29
  54.9 13.5 %collective-permute-start.9 = (f32[64,1024]{1,0:T(8,128)S(1)}, f32[64,1024]{1,0:T(8,128)S(1)}, u32[]{:S(2)}, u32[]{:S(2)}) collective-permute-start(f32[64,1024]{1,0:T(8,128)S(1)} %collective-permute-done.5), channel_id=1, source_target_pairs={{0,224},{1,33},{32,0},{33,65},{64,32},{65,97},{96,64},{97,129},{12... | collective-permute-start | bytes 786440 | tf_op jit(solution)/shard_map/ppermute | solution.py:29
  60.0 13.6 %collective-permute-start.10 = (f32[64,1024]{1,0:T(8,128)S(1)}, f32[64,1024]{1,0:T(8,128)S(1)}, u32[]{:S(2)}, u32[]{:S(2)}) collective-permute-start(f32[64,1024]{1,0:T(8,128)S(1)} %collective-permute-done.6), channel_id=1, source_target_pairs={{0,256},{1,263},{32,288},{33,295},{64,320},{65,327},{96,352},{97,3... | collective-permute-start | bytes 786440 | tf_op jit(solution)/shard_map/ppermute | solution.py:29
  62.7 11.5 %collective-permute-start.11 = (f32[64,1024]{1,0:T(8,128)S(1)}, f32[64,1024]{1,0:T(8,128)S(1)}, u32[]{:S(2)}, u32[]{:S(2)}) collective-permute-start(f32[64,1024]{1,0:T(8,128)S(1)} %collective-permute-done.7), channel_id=1, source_target_pairs={{0,32},{1,225},{32,64},{33,1},{64,96},{65,33},{96,128},{97,65},{12... | collective-permute-start | bytes 786440 | tf_op jit(solution)/shard_map/ppermute | solution.py:29
  64.7 9.5 %collective-permute-start.12 = (f32[64,1024]{1,0:T(8,128)S(1)}, f32[64,1024]{1,0:T(8,128)S(1)}, u32[]{:S(2)}, u32[]{:S(2)}) collective-permute-start(f32[64,1024]{1,0:T(8,128)S(1)} %collective-permute-done.8), channel_id=1, source_target_pairs={{0,262},{1,257},{32,294},{33,289},{64,326},{65,321},{96,358},{97,3... | collective-permute-start | bytes 786440 | tf_op jit(solution)/shard_map/ppermute | solution.py:29
  68.4 9.0 %collective-permute-start.13 = (f32[64,1024]{1,0:T(8,128)S(1)}, f32[64,1024]{1,0:T(8,128)S(1)}, u32[]{:S(2)}, u32[]{:S(2)}) collective-permute-start(f32[64,1024]{1,0:T(8,128)S(1)} %collective-permute-done.9), channel_id=1, source_target_pairs={{0,224},{1,33},{32,0},{33,65},{64,32},{65,97},{96,64},{97,129},{12... | collective-permute-start | bytes 786440 | tf_op jit(solution)/shard_map/ppermute | solution.py:29
  80.1 4.0 %collective-permute-start.14 = (f32[32,5,8,128]{3,2,1,0:T(8,128)S(1)}, f32[32,5,8,128]{3,2,1,0:T(8,128)S(1)}, u32[]{:S(2)}, u32[]{:S(2)}) collective-permute-start(f32[32,5,8,128]{3,2,1,0:T(8,128)S(1)} %fusion.1), channel_id=1, source_target_pairs={{0,1},{1,0},{32,33},{33,32},{64,65},{65,64},{96,97},{97,96},{128,1... | collective-permute-start | bytes 1966088 | tf_op jit(solution)/shard_map/ppermute | solution.py:29
  85.0 32.0 %all-to-all-start.1 = ((f32[32,5,8,128]{3,2,1,0:T(8,128)}), f32[32,5,8,128]{3,2,1,0:T(8,128)S(1)}, u32[]{:S(2)}, u32[]{:S(2)}) async-start(f32[32,5,8,128]{3,2,1,0:T(8,128)} %fusion.4), calls=%async_computation.1 | async-start | bytes 1310720 | tf_op jit(solution)/shard_map/all_to_all | solution.py:77

commit v2 on v1

v2 whole, which is shorter than its diff:
```python
import jax
import jax.numpy as jnp
from jax import lax
from jax.experimental import pallas as pl
from jax.experimental.pallas import tpu as pltpu
from jax.sharding import PartitionSpec as P

XS, YH, YL, ZS, CS = 4, 4, 2, 8, 2
YS = YH * YL
FEAT = XS * YH * CS
AXES = ("ex", "feat")
VMEM = pl.BlockSpec(memory_space=pltpu.VMEM)
SMEM = pl.BlockSpec(memory_space=pltpu.SMEM)
PARAMS = pltpu.CompilerParams(vmem_limit_bytes=32 * 1024 * 1024)


def device_at(x, y, z, c):
    return ((y % YL) * ZS + z) * FEAT + x * (YH * CS) + (y // YL) * CS + c


X_GROUPS = [[x * (YH * CS) + yh * CS + c for x in range(XS)] for yh in range(YH) for c in range(CS)]
LEFT_GROUPS = [[device_at(x, yh * YL + yl, z, c) for x in range(XS) for yl in range(YL)]
               for yh in range(YH) for z in range(ZS) for c in range(CS)]
XY_GROUPS = [[device_at(x, y, z, c) for x in range(XS) for y in range(YS)]
             for z in range(ZS) for c in range(CS)]


def shift(value, move):
    pairs = []
    for x in range(XS):
        for y in range(YS):
            for z in range(ZS):
                for c in range(CS):
                    nx, ny, nz, nc = move(x, y, z, c)
                    pairs.append((device_at(x, y, z, c), device_at(nx % XS, ny % YS, nz % ZS, nc % CS)))
    return lax.ppermute(value, AXES, pairs)


def ring(piece, at, sign):
    whole = lax.dynamic_update_slice(jnp.zeros((ZS,) + piece.shape, jnp.float32), piece[None], (at, 0, 0))
    ahead, behind = piece, piece
    for step in range(1, 5):
        ahead = shift(ahead, lambda x, y, z, c: (x, y, z + (-1 if c == 0 else 1), c))
        whole = lax.dynamic_update_slice(whole, ahead[None], ((at + sign * step) % ZS, 0, 0))
        if step < 4:
            behind = shift(behind, lambda x, y, z, c: (x, y, z + (1 if c == 0 else -1), c))
            whole = lax.dynamic_update_slice(whole, behind[None], ((at - sign * step) % ZS, 0, 0))
    return whole.reshape(-1, piece.shape[1])


def scale_kernel(grads_ref, moment_ref, scaled_ref, copies_ref):
    scaled = grads_ref[...] * (1.0 / (jnp.sqrt(moment_ref[...]) + 1e-08))
    scaled_ref[...] = scaled
    for i in range(XS * YL):
        copies_ref[i] = scaled


def scale(grads, second_moment):
    return pl.pallas_call(
        scale_kernel,
        out_shape=(jax.ShapeDtypeStruct((256, 256), jnp.float32),
                   jax.ShapeDtypeStruct((XS * YL, 256, 256), jnp.float32)),
        in_specs=[VMEM, VMEM],
        out_specs=(VMEM, VMEM),
        compiler_params=PARAMS,
        cost_estimate=pl.CostEstimate(flops=65536, bytes_accessed=2621440, transcendentals=256),
    )(grads, second_moment.reshape(1, 256))


def halves(value):
    high = value.astype(jnp.bfloat16)
    return high, (value - high.astype(jnp.float32)).astype(jnp.bfloat16)


def dot_t(left, right):
    return lax.dot_general(left, right, (((1,), (1,)), ((), ())), preferred_element_type=jnp.float32)


def product_kernel(core_ref, left_ref, right_ref, mine_ref, theirs_ref, total_ref):
    ones = jnp.ones((8, 256), jnp.bfloat16)
    sums = jnp.zeros((8, 512), jnp.float32)
    for x in range(XS):
        block = right_ref[:, x * 256:(x + 1) * 256]
        right_high, right_low = halves(block)
        square_high, square_low = halves(block * block)
        sums = sums + dot_t(ones, square_high) + dot_t(ones, square_low)
        for yl in range(YL):
            left_high, left_low = halves(left_ref[x * YL + yl])
            part = dot_t(left_high, right_high) + dot_t(left_high, right_low) + dot_t(left_low, right_high)
            if x == 0:
                total_ref[yl] = part
            else:
                total_ref[yl] += part
    row = lax.broadcasted_iota(jnp.int32, (8, 128), 0)
    tile = jnp.zeros((8, 128), jnp.float32)
    for q in range(4):
        tile = jnp.where(row == q, sums[:, q * 128:(q + 1) * 128], tile)

    def write(refs):
        for x in range(XS):
            for yh in range(YH):
                for yl in range(YL):
                    to = (x * YH + yh) * YL + yl
                    for c in range(CS):
                        at = x * 64 + yh * 16 + c * 8
                        for q in range(4):
                            refs[c][to, q] = total_ref[yl, at:at + 8, q * 128:(q + 1) * 128]
                        refs[c][to, 4] = tile

    @pl.when(core_ref[0] == 0)
    def _():
        write((mine_ref, theirs_ref))

    @pl.when(core_ref[0] == 1)
    def _():
        write((theirs_ref, mine_ref))


def product(core, left, right):
    message = jax.ShapeDtypeStruct((XS * YS, 5, 8, 128), jnp.float32)
    return pl.pallas_call(
        product_kernel,
        out_shape=(message, message),
        in_specs=[SMEM, VMEM, VMEM],
        out_specs=(VMEM, VMEM),
        scratch_shapes=[pltpu.VMEM((YL, 256, 512), jnp.float32)],
        compiler_params=PARAMS,
        cost_estimate=pl.CostEstimate(flops=3 * 2 * 512 * 512 * 1024, bytes_accessed=5505024, transcendentals=0),
    )(core.reshape(1), left, right)


def finish_kernel(place_ref, whole_ref, out_ref, scale_ref):
    row = lax.broadcasted_iota(jnp.int32, (8, 128), 0)
    lane = lax.broadcasted_iota(jnp.int32, (8, 128), 1)
    tiles = {}
    for x in range(XS):
        for yl in range(YL):
            got = [sum(whole_ref[(x * YH + yh) * YL + yl, q] for yh in range(YH)) for q in range(5)]
            factor = lax.rsqrt(got[4] + 1e-06)
            scale_ref[x * YL + yl] = factor
            for q in range(4):
                tiles[x, yl, q] = got[q] * factor[q:q + 1, :]
    x, yl, z, at = place_ref[0], place_ref[1], place_ref[2], place_ref[3]
    own = jnp.where(row == z // 2, scale_ref[x * YL + yl], 0.0)
    own = jnp.sum(own, axis=0, keepdims=True)
    own = jnp.where(lane == row + (z % 2) * 64 + at, own, 0.0)
    own = jnp.sum(own, axis=1, keepdims=True)
    for yl in range(YL):
        for q in range(4):
            for pair in range(2):
                low, high = tiles[2 * pair, yl, q] * own, tiles[2 * pair + 1, yl, q] * own
                even = jnp.where(lane < 64, low, pltpu.roll(high, 64, 1))
                odd = jnp.where(lane < 64, pltpu.roll(low, 64, 1), high)
                start = yl * 2048 + q * 512 + pair * 128
                out_ref[:, start:start + 128] = even
                out_ref[:, start + 256:start + 384] = odd


def finish(place, whole):
    return pl.pallas_call(
        finish_kernel,
        out_shape=jax.ShapeDtypeStruct((8, 4096), jnp.float32),
        in_specs=[SMEM, VMEM],
        out_specs=VMEM,
        scratch_shapes=[pltpu.VMEM((XS * YL, 8, 128), jnp.float32)],
        compiler_params=PARAMS,
        cost_estimate=pl.CostEstimate(flops=262144, bytes_accessed=786432, transcendentals=4096),
    )(place, whole)


def shards(grads, second_moment):
    ex, feat = lax.axis_index("ex"), lax.axis_index("feat")
    z, y_lo = ex % ZS, ex // ZS
    x, y_hi, core = feat // (YH * CS), (feat // CS) % YH, feat % CS

    scaled, copies = scale(grads, second_moment)
    swapped = lax.all_to_all(scaled.reshape(XS, 64, 256), "feat", 0, 0, axis_index_groups=X_GROUPS, tiled=True)
    piece = jnp.transpose(swapped, (1, 0, 2)).reshape(64, XS * 256)
    left = lax.all_to_all(copies, AXES, 0, 0, axis_index_groups=LEFT_GROUPS, tiled=True)
    right = ring(piece, z, 1 - 2 * core)

    mine, theirs = product(core, left, right)
    mine = mine + shift(theirs, lambda x, y, z, c: (x, y, z, c + 1))
    whole = lax.all_to_all(mine, AXES, 0, 0, axis_index_groups=XY_GROUPS, tiled=True)
    return finish(jnp.stack([x, y_lo, z, y_hi * 16 + core * 8]), whole)


def solution(mesh):
    return jax.shard_map(
        shards,
        mesh=mesh,
        in_specs=(P("ex", "feat"), P("feat")),
        out_specs=P(("ex", "feat"), None),
        check_vma=False,
    )
```

time: 119 us -> 107 us (0.90)
  starting transfers between devices: 66.6 us -> 50.2 us
  waiting for transfers between devices: 26.4 us -> 34.7 us
  Pallas kernels: 0 us -> 6.99 us
  blocking collectives: 16.8 us -> 10.8 us
  other arithmetic: 3.88 us -> 0.99 us
  matrix products: 1.85 us -> 0 us
    ppermute x15 -> x8, starting transfers between devices: 55.2 us -> 31.7 us  [shift(): return lax.ppermute(value, AXES, pairs)]
    ppermute x15 -> x8, waiting for transfers between devices: 5.78 us -> 14.3 us  [shift(): return lax.ppermute(value, AXES, pairs)]
    all_to_all x1 -> x2, starting transfers between devices: 11.4 us -> 18.5 us  [the longest x1 10.1 us: shards(): lax.all_to_all(mine, AXES, 0, 0, axis_index_groups=XY_GROUPS, tiled=True)]
    pallas_call x0 -> x3, Pallas kernels: none -> 6.99 us  [the longest x1 4.09 us: product(): pl.pallas_call(product_kernel, out_shape=(message, message), in_specs=[SM...]
    all_to_all x1, blocking collectives: 16.8 us -> 10.8 us  [shards(): lax.all_to_all(scaled.reshape(XS, 64, 256), 'feat', 0, 0, axis_index_grou...]
    dot_general x1 -> x0, matrix products: 1.85 us -> none  [shards(): lax.dot_general(left, right, (((1,), (1,)), ((), ())), precision=lax.Prec...]
    mul x2 -> x0, other arithmetic: 1.72 us -> none  [the longest x1 0.98 us: shards(): scaled = grads * (1.0 / (jnp.sqrt(second_moment) + 1e-08))[None, :]]
    unnamed x0 -> x4, local copies, waits for them, and re-layouts: none -> 1.63 us
  transfers between devices with their start and end apart: 16 -> 10, of which waited for: 4 -> 8; matrix products, arithmetic and copies ran while one was open for 1% -> 1% of each run, Pallas kernels for 0% -> 0%
where the time goes in v2:
time: 107 us; the launch traced here: 106 us
  starting transfers between devices  50.2 us (47%)
  waiting for transfers between devices  34.7 us (32%)
  blocking collectives  10.8 us (10%)
  Pallas kernels  6.99 us (7%)
  local copies, waits for them, and re-layouts  2.38 us (2%)
    ppermute x8, starting transfers between devices, shift(): return lax.ppermute(value, AXES, pairs)  31.7 us
    all_to_all x1, waiting for transfers between devices, shards(): lax.all_to_all(mine, AXES, 0, 0, axis_index_groups=XY_GROUPS, tiled=True)  20.5 us
    ppermute x8, waiting for transfers between devices, shift(): return lax.ppermute(value, AXES, pairs)  14.3 us
    all_to_all x1, blocking collectives, shards(): lax.all_to_all(scaled.reshape(XS, 64, 256), 'feat', 0, 0, axis_index_grou...  10.8 us
    all_to_all x1, starting transfers between devices, shards(): lax.all_to_all(mine, AXES, 0, 0, axis_index_groups=XY_GROUPS, tiled=True)  10.1 us
    all_to_all x1, starting transfers between devices, shards(): lax.all_to_all(copies, AXES, 0, 0, axis_index_groups=LEFT_GROUPS, tiled=T...  8.34 us
    pallas_call x1, Pallas kernels, product(): pl.pallas_call(product_kernel, out_shape=(message, message), in_specs=[SM...  4.09 us
  transfers between devices with their start and end apart: 10, of which 8 were waited for; matrix products, arithmetic and copies ran while one was open for 1% of the time, Pallas kernels for 0%

profile of v2, /device:TPU:8, one launch (start us, length us, event | category | flops | bytes accessed | tf_op | source)
XLA Modules:
  0.0 106.5 jit_solution(519784433866852475)
XLA Ops:
  0.0 0.9 copy-done
  1.6 1.5 %shard_map.28 = (f32[256,256]{1,0:T(8,128)S(1)}, f32[8,256,256]{2,1,0:T(8,128)}) custom-call(f32[256,256]{1,0:T(8,128)S(1)} %copy-done, f32[1,256]{1,0:T(1,128)S(1)} %bitcast.27), custom_call_target="tpu_custom_call" | custom-call | flops 65536 | bytes 2621440 | tf_op jit(solution)/shard_map/pallas_call | solution.py:59
  3.1 10.8 %all_to_all.15 = f32[4,64,256]{2,1,0:T(8,128)S(1)} all-to-all(f32[4,64,256]{2,1,0:T(8,128)S(1)} %bitcast.26), channel_id=1, replica_groups={{0,8,16,24},{1,9,17,25},{2,10,18,26},{3,11,19,27},{4,12,20,28},{5,13,21..., dimensions={0} | all-to-all | bytes 524288 | tf_op jit(solution)/shard_map/all_to_all | solution.py:177
  13.9 8.3 %all-to-all-start = ((f32[8,256,256]{2,1,0:T(8,128)}), f32[8,256,256]{2,1,0:T(8,128)}, u32[]{:S(2)}, u32[]{:S(2)}) async-start(f32[8,256,256]{2,1,0:T(8,128)} %get-tuple-element.9), calls=%async_computation | async-start | bytes 4194304 | tf_op jit(solution)/shard_map/all_to_all | solution.py:179
  22.3 7.3 %collective-permute-start = (f32[64,1024]{1,0:T(8,128)S(1)}, f32[64,1024]{1,0:T(8,128)S(1)}, u32[]{:S(2)}, u32[]{:S(2)}) collective-permute-start(f32[64,1024]{1,0:T(8,128)S(1)} %bitcast.30), channel_id=1, source_target_pairs={{0,224},{1,33},{32,0},{33,65},{64,32},{65,97},{96,64},{97,129},{12... | collective-permute-start | bytes 786440 | tf_op jit(solution)/shard_map/ppermute | solution.py:36
  29.5 1.9 %collective-permute-start.1 = (f32[64,1024]{1,0:T(8,128)S(1)}, f32[64,1024]{1,0:T(8,128)S(1)}, u32[]{:S(2)}, u32[]{:S(2)}) collective-permute-start(f32[64,1024]{1,0:T(8,128)S(1)} %bitcast.31), channel_id=1, source_target_pairs={{0,32},{1,225},{32,64},{33,1},{64,96},{65,33},{96,128},{97,65},{12... | collective-permute-start | bytes 786440 | tf_op jit(solution)/shard_map/ppermute | solution.py:36
  32.2 3.1 %collective-permute-done = f32[64,1024]{1,0:T(8,128)S(1)} collective-permute-done((f32[64,1024]{1,0:T(8,128)S(1)}, f32[64,1024]{1,0:T(8,128)S(1)}, u32[]{:S(2)}, u32[]{:S(2)}) %collective-permute-start) | collective-permute-done | bytes 262176 | tf_op jit(solution)/shard_map/ppermute | solution.py:36
  35.3 5.6 %collective-permute-start.2 = (f32[64,1024]{1,0:T(8,128)S(1)}, f32[64,1024]{1,0:T(8,128)S(1)}, u32[]{:S(2)}, u32[]{:S(2)}) collective-permute-start(f32[64,1024]{1,0:T(8,128)S(1)} %collective-permute-done), channel_id=1, source_target_pairs={{0,224},{1,33},{32,0},{33,65},{64,32},{65,97},{96,64},{97,129},{12... | collective-permute-start | bytes 786440 | tf_op jit(solution)/shard_map/ppermute | solution.py:36
  40.9 1.9 %collective-permute-start.3 = (f32[64,1024]{1,0:T(8,128)S(1)}, f32[64,1024]{1,0:T(8,128)S(1)}, u32[]{:S(2)}, u32[]{:S(2)}) collective-permute-start(f32[64,1024]{1,0:T(8,128)S(1)} %collective-permute-done.1), channel_id=1, source_target_pairs={{0,32},{1,225},{32,64},{33,1},{64,96},{65,33},{96,128},{97,65},{12... | collective-permute-start | bytes 786440 | tf_op jit(solution)/shard_map/ppermute | solution.py:36
  42.9 3.0 %collective-permute-done.2 = f32[64,1024]{1,0:T(8,128)S(1)} collective-permute-done((f32[64,1024]{1,0:T(8,128)S(1)}, f32[64,1024]{1,0:T(8,128)S(1)}, u32[]{:S(2)}, u32[]{:S(2)}) %collective-permute-start.2) | collective-permute-done | bytes 262176 | tf_op jit(solution)/shard_map/ppermute | solution.py:36
  46.0 5.6 %collective-permute-start.4 = (f32[64,1024]{1,0:T(8,128)S(1)}, f32[64,1024]{1,0:T(8,128)S(1)}, u32[]{:S(2)}, u32[]{:S(2)}) collective-permute-start(f32[64,1024]{1,0:T(8,128)S(1)} %collective-permute-done.2), channel_id=1, source_target_pairs={{0,224},{1,33},{32,0},{33,65},{64,32},{65,97},{96,64},{97,129},{12... | collective-permute-start | bytes 786440 | tf_op jit(solution)/shard_map/ppermute | solution.py:36
  51.6 1.5 %collective-permute-done.3 = f32[64,1024]{1,0:T(8,128)S(1)} collective-permute-done((f32[64,1024]{1,0:T(8,128)S(1)}, f32[64,1024]{1,0:T(8,128)S(1)}, u32[]{:S(2)}, u32[]{:S(2)}) %collective-permute-start.3) | collective-permute-done | bytes 262176 | tf_op jit(solution)/shard_map/ppermute | solution.py:36
  53.1 1.9 %collective-permute-start.5 = (f32[64,1024]{1,0:T(8,128)S(1)}, f32[64,1024]{1,0:T(8,128)S(1)}, u32[]{:S(2)}, u32[]{:S(2)}) collective-permute-start(f32[64,1024]{1,0:T(8,128)S(1)} %collective-permute-done.3), channel_id=1, source_target_pairs={{0,32},{1,225},{32,64},{33,1},{64,96},{65,33},{96,128},{97,65},{12... | collective-permute-start | bytes 786440 | tf_op jit(solution)/shard_map/ppermute | solution.py:36
  55.1 0.7 collective-permute-done.4
  55.8 5.6 %collective-permute-start.6 = (f32[64,1024]{1,0:T(8,128)S(1)}, f32[64,1024]{1,0:T(8,128)S(1)}, u32[]{:S(2)}, u32[]{:S(2)}) collective-permute-start(f32[64,1024]{1,0:T(8,128)S(1)} %collective-permute-done.4), channel_id=1, source_target_pairs={{0,224},{1,33},{32,0},{33,65},{64,32},{65,97},{96,64},{97,129},{12... | collective-permute-start | bytes 786440 | tf_op jit(solution)/shard_map/ppermute | solution.py:36
  61.4 3.1 %collective-permute-done.5 = f32[64,1024]{1,0:T(8,128)S(1)} collective-permute-done((f32[64,1024]{1,0:T(8,128)S(1)}, f32[64,1024]{1,0:T(8,128)S(1)}, u32[]{:S(2)}, u32[]{:S(2)}) %collective-permute-start.5) | collective-permute-done | bytes 262176 | tf_op jit(solution)/shard_map/ppermute | solution.py:36
  64.5 0.7 collective-permute-done.6
  65.3 4.1 %shard_map.29 = (f32[32,5,8,128]{3,2,1,0:T(8,128)S(1)}, f32[32,5,8,128]{3,2,1,0:T(8,128)S(1)}) custom-call(s32[1]{0:T(128)} %bitcast.4.core_ref, f32[8,256,256]{2,1,0:T(8,128)} %all-to-all-done.left_ref, f32[512,1024]{1,0:T(8,128)S(1)} %bitcast.25), custom_call_target="tpu_custom_call" | custom-call | flops 1610612736 | bytes 5505024 | tf_op jit(solution)/shard_map/pallas_call | solution.py:121
  69.4 1.9 %collective-permute-start.7 = (f32[32,5,8,128]{3,2,1,0:T(8,128)S(1)}, f32[32,5,8,128]{3,2,1,0:T(8,128)S(1)}, u32[]{:S(2)}, u32[]{:S(2)}) collective-permute-start(f32[32,5,8,128]{3,2,1,0:T(8,128)S(1)} %get-tuple-element.12), channel_id=1, source_target_pairs={{0,1},{1,0},{32,33},{33,32},{64,65},{65,64},{96,97},{97,96},{128,1... | collective-permute-start | bytes 1966088 | tf_op jit(solution)/shard_map/ppermute | solution.py:36
  71.3 2.1 %collective-permute-done.7 = f32[32,5,8,128]{3,2,1,0:T(8,128)S(1)} collective-permute-done((f32[32,5,8,128]{3,2,1,0:T(8,128)S(1)}, f32[32,5,8,128]{3,2,1,0:T(8,128)S(1)}, u32[]{:S(2)}, u32[]{:S(2)}) %collective-permute-start.7) | collective-permute-done | bytes 655392 | tf_op jit(solution)/shard_map/ppermute | solution.py:36
  73.4 0.9 add.99
  74.3 10.1 %all-to-all-start.2 = ((f32[32,5,8,128]{3,2,1,0:T(8,128)}), f32[32,5,8,128]{3,2,1,0:T(8,128)S(1)}, u32[]{:S(2)}, u32[]{:S(2)}) async-start(f32[32,5,8,128]{3,2,1,0:T(8,128)} %add.99), calls=%async_computation.2 | async-start | bytes 1310720 | tf_op jit(solution)/shard_map/all_to_all | solution.py:184
  84.6 20.5 %all-to-all-done.2.whole_ref = f32[32,5,8,128]{3,2,1,0:T(8,128)S(1)} async-done(((f32[32,5,8,128]{3,2,1,0:T(8,128)}), f32[32,5,8,128]{3,2,1,0:T(8,128)S(1)}, u32[]{:S(2)}, u32[]{:S(2)}) %all-to-all-start.2) | async-done | bytes 655392 | tf_op jit(solution)/shard_map/all_to_all | solution.py:184
  105.1 1.4 %shard_map.30 = f32[8,4096]{1,0:T(8,128)} custom-call(s32[4]{0:T(128)S(1)} %pad_add_fusion.place_ref, f32[32,5,8,128]{3,2,1,0:T(8,128)S(1)} %all-to-all-done.2.whole_ref), custom_call_target="tpu_custom_call" | custom-call | flops 262144 | bytes 786432 | tf_op jit(solution)/shard_map/pallas_call | solution.py:160
  (18 shorter events, 1.5 us)
Async XLA Ops:
  0.0 0.9 copy-start
  1.0 0.7 copy-start.1
  13.9 51.4 %all-to-all-start = ((f32[8,256,256]{2,1,0:T(8,128)}), f32[8,256,256]{2,1,0:T(8,128)}, u32[]{:S(2)}, u32[]{:S(2)}) async-start(f32[8,256,256]{2,1,0:T(8,128)} %get-tuple-element.9), calls=%async_computation | async-start | bytes 4194304 | tf_op jit(solution)/shard_map/all_to_all | solution.py:179
  22.3 13.1 %collective-permute-start = (f32[64,1024]{1,0:T(8,128)S(1)}, f32[64,1024]{1,0:T(8,128)S(1)}, u32[]{:S(2)}, u32[]{:S(2)}) collective-permute-start(f32[64,1024]{1,0:T(8,128)S(1)} %bitcast.30), channel_id=1, source_target_pairs={{0,224},{1,33},{32,0},{33,65},{64,32},{65,97},{96,64},{97,129},{12... | collective-permute-start | bytes 786440 | tf_op jit(solution)/shard_map/ppermute | solution.py:36
  29.5 11.4 %collective-permute-start.1 = (f32[64,1024]{1,0:T(8,128)S(1)}, f32[64,1024]{1,0:T(8,128)S(1)}, u32[]{:S(2)}, u32[]{:S(2)}) collective-permute-start(f32[64,1024]{1,0:T(8,128)S(1)} %bitcast.31), channel_id=1, source_target_pairs={{0,32},{1,225},{32,64},{33,1},{64,96},{65,33},{96,128},{97,65},{12... | collective-permute-start | bytes 786440 | tf_op jit(solution)/shard_map/ppermute | solution.py:36
  35.3 10.6 %collective-permute-start.2 = (f32[64,1024]{1,0:T(8,128)S(1)}, f32[64,1024]{1,0:T(8,128)S(1)}, u32[]{:S(2)}, u32[]{:S(2)}) collective-permute-start(f32[64,1024]{1,0:T(8,128)S(1)} %collective-permute-done), channel_id=1, source_target_pairs={{0,224},{1,33},{32,0},{33,65},{64,32},{65,97},{96,64},{97,129},{12... | collective-permute-start | bytes 786440 | tf_op jit(solution)/shard_map/ppermute | solution.py:36
  40.9 12.2 %collective-permute-start.3 = (f32[64,1024]{1,0:T(8,128)S(1)}, f32[64,1024]{1,0:T(8,128)S(1)}, u32[]{:S(2)}, u32[]{:S(2)}) collective-permute-start(f32[64,1024]{1,0:T(8,128)S(1)} %collective-permute-done.1), channel_id=1, source_target_pairs={{0,32},{1,225},{32,64},{33,1},{64,96},{65,33},{96,128},{97,65},{12... | collective-permute-start | bytes 786440 | tf_op jit(solution)/shard_map/ppermute | solution.py:36
  46.0 9.8 %collective-permute-start.4 = (f32[64,1024]{1,0:T(8,128)S(1)}, f32[64,1024]{1,0:T(8,128)S(1)}, u32[]{:S(2)}, u32[]{:S(2)}) collective-permute-start(f32[64,1024]{1,0:T(8,128)S(1)} %collective-permute-done.2), channel_id=1, source_target_pairs={{0,224},{1,33},{32,0},{33,65},{64,32},{65,97},{96,64},{97,129},{12... | collective-permute-start | bytes 786440 | tf_op jit(solution)/shard_map/ppermute | solution.py:36
  53.1 11.4 %collective-permute-start.5 = (f32[64,1024]{1,0:T(8,128)S(1)}, f32[64,1024]{1,0:T(8,128)S(1)}, u32[]{:S(2)}, u32[]{:S(2)}) collective-permute-start(f32[64,1024]{1,0:T(8,128)S(1)} %collective-permute-done.3), channel_id=1, source_target_pairs={{0,32},{1,225},{32,64},{33,1},{64,96},{65,33},{96,128},{97,65},{12... | collective-permute-start | bytes 786440 | tf_op jit(solution)/shard_map/ppermute | solution.py:36
  55.8 9.5 %collective-permute-start.6 = (f32[64,1024]{1,0:T(8,128)S(1)}, f32[64,1024]{1,0:T(8,128)S(1)}, u32[]{:S(2)}, u32[]{:S(2)}) collective-permute-start(f32[64,1024]{1,0:T(8,128)S(1)} %collective-permute-done.4), channel_id=1, source_target_pairs={{0,224},{1,33},{32,0},{33,65},{64,32},{65,97},{96,64},{97,129},{12... | collective-permute-start | bytes 786440 | tf_op jit(solution)/shard_map/ppermute | solution.py:36
  69.4 4.0 %collective-permute-start.7 = (f32[32,5,8,128]{3,2,1,0:T(8,128)S(1)}, f32[32,5,8,128]{3,2,1,0:T(8,128)S(1)}, u32[]{:S(2)}, u32[]{:S(2)}) collective-permute-start(f32[32,5,8,128]{3,2,1,0:T(8,128)S(1)} %get-tuple-element.12), channel_id=1, source_target_pairs={{0,1},{1,0},{32,33},{33,32},{64,65},{65,64},{96,97},{97,96},{128,1... | collective-permute-start | bytes 1966088 | tf_op jit(solution)/shard_map/ppermute | solution.py:36
  74.3 30.8 %all-to-all-start.2 = ((f32[32,5,8,128]{3,2,1,0:T(8,128)}), f32[32,5,8,128]{3,2,1,0:T(8,128)S(1)}, u32[]{:S(2)}, u32[]{:S(2)}) async-start(f32[32,5,8,128]{3,2,1,0:T(8,128)} %add.99), calls=%async_computation.2 | async-start | bytes 1310720 | tf_op jit(solution)/shard_map/all_to_all | solution.py:184

commit v3 on v2

v3 whole, which is shorter than its diff:
```python
import jax
import jax.numpy as jnp
from jax import lax
from jax.experimental import pallas as pl
from jax.experimental.pallas import tpu as pltpu
from jax.sharding import PartitionSpec as P

XS, YH, YL, ZS, CS = 4, 4, 2, 8, 2
YS = YH * YL
FEAT = XS * YH * CS
AXES = ("ex", "feat")
VMEM = pl.BlockSpec(memory_space=pltpu.VMEM)
SMEM = pl.BlockSpec(memory_space=pltpu.SMEM)
PARAMS = pltpu.CompilerParams(vmem_limit_bytes=32 * 1024 * 1024)


def device_at(x, y, z, c):
    return ((y % YL) * ZS + z) * FEAT + x * (YH * CS) + (y // YL) * CS + c


X_GROUPS = [[x * (YH * CS) + yh * CS + c for x in range(XS)] for yh in range(YH) for c in range(CS)]
LEFT_GROUPS = [[device_at(x, yh * YL + yl, z, c) for x in range(XS) for yl in range(YL)]
               for yh in range(YH) for z in range(ZS) for c in range(CS)]
XY_GROUPS = [[device_at(x, y, z, c) for x in range(XS) for y in range(YS)]
             for z in range(ZS) for c in range(CS)]


def shift(value, move):
    pairs = []
    for x in range(XS):
        for y in range(YS):
            for z in range(ZS):
                for c in range(CS):
                    nx, ny, nz, nc = move(x, y, z, c)
                    pairs.append((device_at(x, y, z, c), device_at(nx % XS, ny % YS, nz % ZS, nc % CS)))
    return lax.ppermute(value, AXES, pairs)


def ring(piece, at, sign, left):
    whole = lax.dynamic_update_slice(jnp.zeros((ZS,) + piece.shape, jnp.float32), piece[None], (at, 0, 0))
    ahead, behind = piece, piece
    for step in range(1, 5):
        if step == 4:
            ahead, left = lax.optimization_barrier((ahead, left))
        ahead = shift(ahead, lambda x, y, z, c: (x, y, z + (-1 if c == 0 else 1), c))
        whole = lax.dynamic_update_slice(whole, ahead[None], ((at + sign * step) % ZS, 0, 0))
        if step < 4:
            behind = shift(behind, lambda x, y, z, c: (x, y, z + (1 if c == 0 else -1), c))
            whole = lax.dynamic_update_slice(whole, behind[None], ((at - sign * step) % ZS, 0, 0))
    return whole.reshape(-1, piece.shape[1]), left


def copies_kernel(value_ref, copies_ref):
    for i in range(XS * YL):
        copies_ref[i] = value_ref[...]


def copies_of(value):
    return pl.pallas_call(
        copies_kernel,
        out_shape=jax.ShapeDtypeStruct((XS * YL, 256, 256), jnp.float32),
        in_specs=[VMEM],
        out_specs=VMEM,
        compiler_params=PARAMS,
        cost_estimate=pl.CostEstimate(flops=0, bytes_accessed=2359296, transcendentals=0),
    )(value)


def panel_kernel(blocks_ref, panel_ref):
    for x in range(XS):
        for yl in range(YL):
            panel_ref[yl * 256:(yl + 1) * 256, x * 256:(x + 1) * 256] = blocks_ref[x * YL + yl]


def panel_of(blocks):
    return pl.pallas_call(
        panel_kernel,
        out_shape=jax.ShapeDtypeStruct((YL * 256, XS * 256), jnp.float32),
        in_specs=[VMEM],
        out_specs=VMEM,
        compiler_params=PARAMS,
        cost_estimate=pl.CostEstimate(flops=0, bytes_accessed=4194304, transcendentals=0),
    )(blocks)


def finish_kernel(place_ref, whole_ref, out_ref, scale_ref):
    row = lax.broadcasted_iota(jnp.int32, (8, 128), 0)
    lane = lax.broadcasted_iota(jnp.int32, (8, 128), 1)
    tiles = {}
    for x in range(XS):
        for yl in range(YL):
            got = [sum(whole_ref[(x * YH + yh) * YL + yl, q] for yh in range(YH)) for q in range(5)]
            factor = lax.rsqrt(got[4] + 1e-06)
            scale_ref[x * YL + yl] = factor
            for q in range(4):
                tiles[x, yl, q] = got[q] * factor[q:q + 1, :]
    x, yl, z, at = place_ref[0], place_ref[1], place_ref[2], place_ref[3]
    own = jnp.where(row == z // 2, scale_ref[x * YL + yl], 0.0)
    own = jnp.sum(own, axis=0, keepdims=True)
    own = jnp.where(lane == row + (z % 2) * 64 + at, own, 0.0)
    own = jnp.sum(own, axis=1, keepdims=True)
    for yl in range(YL):
        for q in range(4):
            for pair in range(2):
                low, high = tiles[2 * pair, yl, q] * own, tiles[2 * pair + 1, yl, q] * own
                even = jnp.where(lane < 64, low, pltpu.roll(high, 64, 1))
                odd = jnp.where(lane < 64, pltpu.roll(low, 64, 1), high)
                start = yl * 2048 + q * 512 + pair * 128
                out_ref[:, start:start + 128] = even
                out_ref[:, start + 256:start + 384] = odd


def finish(place, whole):
    return pl.pallas_call(
        finish_kernel,
        out_shape=jax.ShapeDtypeStruct((8, 4096), jnp.float32),
        in_specs=[SMEM, VMEM],
        out_specs=VMEM,
        scratch_shapes=[pltpu.VMEM((XS * YL, 8, 128), jnp.float32)],
        compiler_params=PARAMS,
        cost_estimate=pl.CostEstimate(flops=262144, bytes_accessed=786432, transcendentals=4096),
    )(place, whole)


def shards(grads, second_moment):
    ex, feat = lax.axis_index("ex"), lax.axis_index("feat")
    z, y_lo = ex % ZS, ex // ZS
    x, y_hi, core = feat // (YH * CS), (feat // CS) % YH, feat % CS

    scaled = grads * (1.0 / (jnp.sqrt(second_moment) + 1e-08))[None, :]
    swapped = lax.all_to_all(scaled.reshape(XS, 64, 256), "feat", 0, 0, axis_index_groups=X_GROUPS, tiled=True)
    piece = jnp.transpose(swapped, (1, 0, 2)).reshape(64, XS * 256)
    scaled, piece = lax.optimization_barrier((scaled, piece))
    blocks = lax.all_to_all(copies_of(scaled), AXES, 0, 0, axis_index_groups=LEFT_GROUPS, tiled=True)
    right, left = ring(piece, z, 1 - 2 * core, panel_of(blocks))

    part = lax.dot_general(left, right, (((1,), (1,)), ((), ())), precision=lax.Precision.HIGH,
                           preferred_element_type=jnp.float32)
    sums = jnp.sum(right * right, axis=1)
    part = jnp.transpose(part.reshape(YL, XS, YH, CS, 8, 4, 128), (3, 1, 2, 0, 5, 4, 6)).reshape(CS, XS * YS, 4, 8, 128)
    sums = jnp.broadcast_to(jnp.pad(sums.reshape(4, 128), ((0, 4), (0, 0))), (CS, XS * YS, 1, 8, 128))
    part = jnp.concatenate([part, sums], axis=2)
    take = lambda i: lax.dynamic_index_in_dim(part, i, 0, keepdims=False)
    mine = take(core) + shift(take(1 - core), lambda x, y, z, c: (x, y, z, c + 1))
    whole = lax.all_to_all(mine, AXES, 0, 0, axis_index_groups=XY_GROUPS, tiled=True)
    return finish(jnp.stack([x, y_lo, z, y_hi * 16 + core * 8]), whole)


def solution(mesh):
    return jax.shard_map(
        shards,
        mesh=mesh,
        in_specs=(P("ex", "feat"), P("feat")),
        out_specs=P(("ex", "feat"), None),
        check_vma=False,
    )
```

time: 107 us -> 109 us (1.019)
  local copies, waits for them, and re-layouts: 2.38 us -> 8.9 us
  Pallas kernels: 6.99 us -> 1.69 us
  waiting for transfers between devices: 34.7 us -> 29.6 us
  other arithmetic: 0.99 us -> 4.51 us
  matrix products: 0 us -> 3.42 us
  starting transfers between devices: 50.2 us -> 49 us
    pallas_call x2, Pallas kernels: 5.59 us -> 0.29 us  [the longest x1 0.15 us: panel_of(): pl.pallas_call(panel_kernel, out_shape=jax.ShapeDtypeStruct((YL * 256, XS...]
    ppermute x8, waiting for transfers between devices: 14.3 us -> 9.15 us  [shift(): return lax.ppermute(value, AXES, pairs)]
    dot_general x0 -> x1, matrix products: none -> 3.42 us  [shards(): lax.dot_general(left, right, (((1,), (1,)), ((), ())), precision=lax.Prec...]
    dynamic_update_slice x4, local copies, waits for them, and re-layouts: 0.09 us -> 2.9 us  [ring(): lax.dynamic_update_slice(whole, ahead[None], ((at + sign * step) % ZS, 0,...]
    dynamic_update_slice x3, local copies, waits for them, and re-layouts: 0.07 us -> 2.16 us  [ring(): lax.dynamic_update_slice(whole, behind[None], ((at - sign * step) % ZS, 0...]
    reduce_sum x0 -> x1, other arithmetic: none -> 1.8 us  [shards(): sums = jnp.sum(right * right, axis=1)]
    broadcast_in_dim x1, local copies, waits for them, and re-layouts: 0.24 us -> 1.58 us  [ring(): jnp.zeros((ZS,) + piece.shape, jnp.float32)]
  transfers between devices with their start and end apart: 10 -> 10, of which waited for: 8 -> 7; matrix products, arithmetic and copies ran while one was open for 1% -> 6% of each run, Pallas kernels for 0% -> 0%
where the time goes in v3:
time: 109 us; the launch traced here: 108 us
  starting transfers between devices  49 us (45%)
  waiting for transfers between devices  29.6 us (27%)
  blocking collectives  10.8 us (10%)
  local copies, waits for them, and re-layouts  8.9 us (8%)
  other arithmetic  4.51 us (4%)
  matrix products  3.42 us (3%)
  Pallas kernels  1.69 us (2%)
    ppermute x8, starting transfers between devices, shift(): return lax.ppermute(value, AXES, pairs)  31.2 us
    all_to_all x1, waiting for transfers between devices, shards(): lax.all_to_all(mine, AXES, 0, 0, axis_index_groups=XY_GROUPS, tiled=True)  20.5 us
    all_to_all x1, blocking collectives, shards(): lax.all_to_all(scaled.reshape(XS, 64, 256), 'feat', 0, 0, axis_index_grou...  10.8 us
    all_to_all x1, starting transfers between devices, shards(): lax.all_to_all(mine, AXES, 0, 0, axis_index_groups=XY_GROUPS, tiled=True)  10.1 us
    ppermute x8, waiting for transfers between devices, shift(): return lax.ppermute(value, AXES, pairs)  9.15 us
    all_to_all x1, starting transfers between devices, shards(): lax.all_to_all(copies_of(scaled), AXES, 0, 0, axis_index_groups=LEFT_GROU...  7.62 us
    dot_general x1, matrix products, shards(): lax.dot_general(left, right, (((1,), (1,)), ((), ())), precision=lax.Prec...  3.42 us
    dynamic_update_slice x4, local copies, waits for them, and re-layouts, ring(): lax.dynamic_update_slice(whole, ahead[None], ((at + sign * step) % ZS, 0,...  2.9 us
  transfers between devices with their start and end apart: 10, of which 7 were waited for; matrix products, arithmetic and copies ran while one was open for 6% of the time, Pallas kernels for 0%

profile of v3, /device:TPU:8, one launch (start us, length us, event | category | flops | bytes accessed | tf_op | source)
XLA Modules:
  0.0 108.3 jit_solution(10466096178620236506)
XLA Ops:
  0.7 1.0 broadcast_multiply_fusion.value_ref
  1.7 10.8 %all_to_all.15 = f32[4,64,256]{2,1,0:T(8,128)S(1)} all-to-all(f32[4,64,256]{2,1,0:T(8,128)S(1)} %bitcast.46), channel_id=1, replica_groups={{0,8,16,24},{1,9,17,25},{2,10,18,26},{3,11,19,27},{4,12,20,28},{5,13,21..., dimensions={0} | all-to-all | bytes 524288 | tf_op jit(solution)/shard_map/all_to_all | solution.py:131
  12.6 1.3 %copy-done = f32[8,256,256]{2,1,0:T(8,128)} copy-done((f32[8,256,256]{2,1,0:T(8,128)}, f32[8,256,256]{2,1,0:T(8,128)S(1)}, u32[]{:S(2)}) %copy-start) | copy-done | bytes 2097176
  13.9 7.6 %all-to-all-start.1 = ((f32[8,256,256]{2,1,0:T(8,128)}), f32[8,256,256]{2,1,0:T(8,128)S(1)}, u32[]{:S(2)}, u32[]{:S(2)}) async-start(f32[8,256,256]{2,1,0:T(8,128)} %copy-done), calls=%async_computation.1 | async-start | bytes 4194304 | tf_op jit(solution)/shard_map/all_to_all | solution.py:134
  21.6 7.3 %collective-permute-start = (f32[64,1024]{1,0:T(8,128)S(1)}, f32[64,1024]{1,0:T(8,128)S(1)}, u32[]{:S(2)}, u32[]{:S(2)}) collective-permute-start(f32[64,1024]{1,0:T(8,128)S(1)} %bitcast.49), channel_id=1, source_target_pairs={{0,224},{1,33},{32,0},{33,65},{64,32},{65,97},{96,64},{97,129},{12... | collective-permute-start | bytes 786440 | tf_op jit(solution)/shard_map/ppermute | solution.py:36
  28.8 1.9 %collective-permute-start.3 = (f32[64,1024]{1,0:T(8,128)S(1)}, f32[64,1024]{1,0:T(8,128)S(1)}, u32[]{:S(2)}, u32[]{:S(2)}) collective-permute-start(f32[64,1024]{1,0:T(8,128)S(1)} %bitcast.50), channel_id=1, source_target_pairs={{0,32},{1,225},{32,64},{33,1},{64,96},{65,33},{96,128},{97,65},{12... | collective-permute-start | bytes 786440 | tf_op jit(solution)/shard_map/ppermute | solution.py:36
  30.9 1.6 %broadcast_in_dim.31 = f32[8,64,1024]{2,1,0:T(8,128)} broadcast(f32[]{:T(128)} %constant.115.clone.1), dimensions={} | broadcast | bytes 2097156 | tf_op jit(solution)/shard_map/broadcast_in_dim | solution.py:40
  33.2 1.4 %collective-permute-done = f32[64,1024]{1,0:T(8,128)S(1)} collective-permute-done((f32[64,1024]{1,0:T(8,128)S(1)}, f32[64,1024]{1,0:T(8,128)S(1)}, u32[]{:S(2)}, u32[]{:S(2)}) %collective-permute-start) | collective-permute-done | bytes 262176 | tf_op jit(solution)/shard_map/ppermute | solution.py:36
  34.6 5.6 %collective-permute-start.1 = (f32[64,1024]{1,0:T(8,128)S(1)}, f32[64,1024]{1,0:T(8,128)S(1)}, u32[]{:S(2)}, u32[]{:S(2)}) collective-permute-start(f32[64,1024]{1,0:T(8,128)S(1)} %collective-permute-done), channel_id=1, source_target_pairs={{0,224},{1,33},{32,0},{33,65},{64,32},{65,97},{96,64},{97,129},{12... | collective-permute-start | bytes 786440 | tf_op jit(solution)/shard_map/ppermute | solution.py:36
  40.2 1.9 %collective-permute-start.4 = (f32[64,1024]{1,0:T(8,128)S(1)}, f32[64,1024]{1,0:T(8,128)S(1)}, u32[]{:S(2)}, u32[]{:S(2)}) collective-permute-start(f32[64,1024]{1,0:T(8,128)S(1)} %collective-permute-done.3), channel_id=1, source_target_pairs={{0,32},{1,225},{32,64},{33,1},{64,96},{65,33},{96,128},{97,65},{12... | collective-permute-start | bytes 786440 | tf_op jit(solution)/shard_map/ppermute | solution.py:36
  43.6 1.6 %collective-permute-done.1 = f32[64,1024]{1,0:T(8,128)S(1)} collective-permute-done((f32[64,1024]{1,0:T(8,128)S(1)}, f32[64,1024]{1,0:T(8,128)S(1)}, u32[]{:S(2)}, u32[]{:S(2)}) %collective-permute-start.1) | collective-permute-done | bytes 262176 | tf_op jit(solution)/shard_map/ppermute | solution.py:36
  45.2 5.6 %collective-permute-start.2 = (f32[64,1024]{1,0:T(8,128)S(1)}, f32[64,1024]{1,0:T(8,128)S(1)}, u32[]{:S(2)}, u32[]{:S(2)}) collective-permute-start(f32[64,1024]{1,0:T(8,128)S(1)} %collective-permute-done.1), channel_id=1, source_target_pairs={{0,224},{1,33},{32,0},{33,65},{64,32},{65,97},{96,64},{97,129},{12... | collective-permute-start | bytes 786440 | tf_op jit(solution)/shard_map/ppermute | solution.py:36
  50.8 1.7 %collective-permute-done.4 = f32[64,1024]{1,0:T(8,128)S(1)} collective-permute-done((f32[64,1024]{1,0:T(8,128)S(1)}, f32[64,1024]{1,0:T(8,128)S(1)}, u32[]{:S(2)}, u32[]{:S(2)}) %collective-permute-start.4) | collective-permute-done | bytes 262176 | tf_op jit(solution)/shard_map/ppermute | solution.py:36
  52.5 1.9 %collective-permute-start.5 = (f32[64,1024]{1,0:T(8,128)S(1)}, f32[64,1024]{1,0:T(8,128)S(1)}, u32[]{:S(2)}, u32[]{:S(2)}) collective-permute-start(f32[64,1024]{1,0:T(8,128)S(1)} %collective-permute-done.4), channel_id=1, source_target_pairs={{0,32},{1,225},{32,64},{33,1},{64,96},{65,33},{96,128},{97,65},{12... | collective-permute-start | bytes 786440 | tf_op jit(solution)/shard_map/ppermute | solution.py:36
  56.0 5.1 %collective-permute-start.6 = (f32[64,1024]{1,0:T(8,128)S(1)}, f32[64,1024]{1,0:T(8,128)S(1)}, u32[]{:S(2)}, u32[]{:S(2)}) collective-permute-start(f32[64,1024]{1,0:T(8,128)S(1)} %collective-permute-done.2), channel_id=1, source_target_pairs={{0,224},{1,33},{32,0},{33,65},{64,32},{65,97},{96,64},{97,129},{12... | collective-permute-start | bytes 786440 | tf_op jit(solution)/shard_map/ppermute | solution.py:36
  61.9 2.0 %collective-permute-done.5 = f32[64,1024]{1,0:T(8,128)S(1)} collective-permute-done((f32[64,1024]{1,0:T(8,128)S(1)}, f32[64,1024]{1,0:T(8,128)S(1)}, u32[]{:S(2)}, u32[]{:S(2)}) %collective-permute-start.5) | collective-permute-done | bytes 262176 | tf_op jit(solution)/shard_map/ppermute | solution.py:36
  65.8 1.8 %multiply_reduce_fusion = f32[8,64]{1,0:T(8,128)S(1)} fusion(f32[8,64,1024]{2,1,0:T(8,128)} %bitcast_dynamic-update-slice_fusion), kind=kLoop, calls=%fused_computation | loop fusion | flops 1048064 | bytes 2099200 | tf_op jit(solution)/shard_map/reduce_sum | solution.py:139
  67.6 3.4 %convolution_bitcast_fusion = f32[2,4,4,2,4,8,128]{6,5,4,0,2,1,3:T(8,128)S(1)} fusion(f32[2,4,4,2,8,1024,1]{5,4,6,3,2,1,0:T(8,128)S(1)} %bitcast.45, f32[4,128,1024,1,1,1,1]{2,1,0,6,5,4,3:T(8,128)} %bitcast.19), kind=kOutput, calls=%fused_computation.3 | convolution fusion | flops 1610612736 | bytes 5242880 | tf_op jit(solution)/shard_map/dot_general | solution.py:137
  71.3 1.9 %collective-permute-start.7 = (f32[32,5,8,128]{3,2,1,0:T(8,128)S(1)}, f32[32,5,8,128]{3,2,1,0:T(8,128)S(1)}, u32[]{:S(2)}, u32[]{:S(2)}) collective-permute-start(f32[32,5,8,128]{3,2,1,0:T(8,128)S(1)} %fusion.1), channel_id=1, source_target_pairs={{0,1},{1,0},{32,33},{33,32},{64,65},{65,64},{96,97},{97,96},{128,1... | collective-permute-start | bytes 1966088 | tf_op jit(solution)/shard_map/ppermute | solution.py:36
  73.2 2.1 %collective-permute-done.7 = f32[32,5,8,128]{3,2,1,0:T(8,128)S(1)} collective-permute-done((f32[32,5,8,128]{3,2,1,0:T(8,128)S(1)}, f32[32,5,8,128]{3,2,1,0:T(8,128)S(1)}, u32[]{:S(2)}, u32[]{:S(2)}) %collective-permute-start.7) | collective-permute-done | bytes 655392 | tf_op jit(solution)/shard_map/ppermute | solution.py:36
  75.3 0.9 fusion.4
  76.2 10.1 %all-to-all-start.2 = ((f32[32,5,8,128]{3,2,1,0:T(8,128)}), f32[32,5,8,128]{3,2,1,0:T(8,128)S(1)}, u32[]{:S(2)}, u32[]{:S(2)}) async-start(f32[32,5,8,128]{3,2,1,0:T(8,128)} %fusion.4), calls=%async_computation.2 | async-start | bytes 1310720 | tf_op jit(solution)/shard_map/all_to_all | solution.py:145
  86.4 20.5 %all-to-all-done.2.whole_ref = f32[32,5,8,128]{3,2,1,0:T(8,128)S(1)} async-done(((f32[32,5,8,128]{3,2,1,0:T(8,128)}), f32[32,5,8,128]{3,2,1,0:T(8,128)S(1)}, u32[]{:S(2)}, u32[]{:S(2)}) %all-to-all-start.2) | async-done | bytes 655392 | tf_op jit(solution)/shard_map/all_to_all | solution.py:145
  106.9 1.4 %shard_map.30 = f32[8,4096]{1,0:T(8,128)} custom-call(s32[4]{0:T(128)S(1)} %pad_add_fusion.place_ref, f32[32,5,8,128]{3,2,1,0:T(8,128)S(1)} %all-to-all-done.2.whole_ref), custom_call_target="tpu_custom_call" | custom-call | flops 262144 | bytes 786432 | tf_op jit(solution)/shard_map/pallas_call | solution.py:114
  (23 shorter events, 7.5 us)
Async XLA Ops:
  12.6 1.3 %copy-start = (f32[8,256,256]{2,1,0:T(8,128)}, f32[8,256,256]{2,1,0:T(8,128)S(1)}, u32[]{:S(2)}) copy-start(f32[8,256,256]{2,1,0:T(8,128)S(1)} %shard_map.28) | copy-start | bytes 6291460
  13.9 41.9 %all-to-all-start.1 = ((f32[8,256,256]{2,1,0:T(8,128)}), f32[8,256,256]{2,1,0:T(8,128)S(1)}, u32[]{:S(2)}, u32[]{:S(2)}) async-start(f32[8,256,256]{2,1,0:T(8,128)} %copy-done), calls=%async_computation.1 | async-start | bytes 4194304 | tf_op jit(solution)/shard_map/all_to_all | solution.py:134
  21.6 13.1 %collective-permute-start = (f32[64,1024]{1,0:T(8,128)S(1)}, f32[64,1024]{1,0:T(8,128)S(1)}, u32[]{:S(2)}, u32[]{:S(2)}) collective-permute-start(f32[64,1024]{1,0:T(8,128)S(1)} %bitcast.49), channel_id=1, source_target_pairs={{0,224},{1,33},{32,0},{33,65},{64,32},{65,97},{96,64},{97,129},{12... | collective-permute-start | bytes 786440 | tf_op jit(solution)/shard_map/ppermute | solution.py:36
  28.8 11.4 %collective-permute-start.3 = (f32[64,1024]{1,0:T(8,128)S(1)}, f32[64,1024]{1,0:T(8,128)S(1)}, u32[]{:S(2)}, u32[]{:S(2)}) collective-permute-start(f32[64,1024]{1,0:T(8,128)S(1)} %bitcast.50), channel_id=1, source_target_pairs={{0,32},{1,225},{32,64},{33,1},{64,96},{65,33},{96,128},{97,65},{12... | collective-permute-start | bytes 786440 | tf_op jit(solution)/shard_map/ppermute | solution.py:36
  34.6 10.5 %collective-permute-start.1 = (f32[64,1024]{1,0:T(8,128)S(1)}, f32[64,1024]{1,0:T(8,128)S(1)}, u32[]{:S(2)}, u32[]{:S(2)}) collective-permute-start(f32[64,1024]{1,0:T(8,128)S(1)} %collective-permute-done), channel_id=1, source_target_pairs={{0,224},{1,33},{32,0},{33,65},{64,32},{65,97},{96,64},{97,129},{12... | collective-permute-start | bytes 786440 | tf_op jit(solution)/shard_map/ppermute | solution.py:36
  40.2 12.3 %collective-permute-start.4 = (f32[64,1024]{1,0:T(8,128)S(1)}, f32[64,1024]{1,0:T(8,128)S(1)}, u32[]{:S(2)}, u32[]{:S(2)}) collective-permute-start(f32[64,1024]{1,0:T(8,128)S(1)} %collective-permute-done.3), channel_id=1, source_target_pairs={{0,32},{1,225},{32,64},{33,1},{64,96},{65,33},{96,128},{97,65},{12... | collective-permute-start | bytes 786440 | tf_op jit(solution)/shard_map/ppermute | solution.py:36
  45.2 10.9 %collective-permute-start.2 = (f32[64,1024]{1,0:T(8,128)S(1)}, f32[64,1024]{1,0:T(8,128)S(1)}, u32[]{:S(2)}, u32[]{:S(2)}) collective-permute-start(f32[64,1024]{1,0:T(8,128)S(1)} %collective-permute-done.1), channel_id=1, source_target_pairs={{0,224},{1,33},{32,0},{33,65},{64,32},{65,97},{96,64},{97,129},{12... | collective-permute-start | bytes 786440 | tf_op jit(solution)/shard_map/ppermute | solution.py:36
  52.5 11.4 %collective-permute-start.5 = (f32[64,1024]{1,0:T(8,128)S(1)}, f32[64,1024]{1,0:T(8,128)S(1)}, u32[]{:S(2)}, u32[]{:S(2)}) collective-permute-start(f32[64,1024]{1,0:T(8,128)S(1)} %collective-permute-done.4), channel_id=1, source_target_pairs={{0,32},{1,225},{32,64},{33,1},{64,96},{65,33},{96,128},{97,65},{12... | collective-permute-start | bytes 786440 | tf_op jit(solution)/shard_map/ppermute | solution.py:36
  56.0 9.0 %collective-permute-start.6 = (f32[64,1024]{1,0:T(8,128)S(1)}, f32[64,1024]{1,0:T(8,128)S(1)}, u32[]{:S(2)}, u32[]{:S(2)}) collective-permute-start(f32[64,1024]{1,0:T(8,128)S(1)} %collective-permute-done.2), channel_id=1, source_target_pairs={{0,224},{1,33},{32,0},{33,65},{64,32},{65,97},{96,64},{97,129},{12... | collective-permute-start | bytes 786440 | tf_op jit(solution)/shard_map/ppermute | solution.py:36
  71.3 4.0 %collective-permute-start.7 = (f32[32,5,8,128]{3,2,1,0:T(8,128)S(1)}, f32[32,5,8,128]{3,2,1,0:T(8,128)S(1)}, u32[]{:S(2)}, u32[]{:S(2)}) collective-permute-start(f32[32,5,8,128]{3,2,1,0:T(8,128)S(1)} %fusion.1), channel_id=1, source_target_pairs={{0,1},{1,0},{32,33},{33,32},{64,65},{65,64},{96,97},{97,96},{128,1... | collective-permute-start | bytes 1966088 | tf_op jit(solution)/shard_map/ppermute | solution.py:36
  76.2 30.8 %all-to-all-start.2 = ((f32[32,5,8,128]{3,2,1,0:T(8,128)}), f32[32,5,8,128]{3,2,1,0:T(8,128)S(1)}, u32[]{:S(2)}, u32[]{:S(2)}) async-start(f32[32,5,8,128]{3,2,1,0:T(8,128)} %fusion.4), calls=%async_computation.2 | async-start | bytes 1310720 | tf_op jit(solution)/shard_map/all_to_all | solution.py:145

commit v4 on v2

--- a/solution.py
+++ b/solution.py
@@ -41,30 +41,28 @@
     ahead, behind = piece, piece
     for step in range(1, 5):
         ahead = shift(ahead, lambda x, y, z, c: (x, y, z + (-1 if c == 0 else 1), c))
+        first = ahead if step == 1 else first
         whole = lax.dynamic_update_slice(whole, ahead[None], ((at + sign * step) % ZS, 0, 0))
         if step < 4:
             behind = shift(behind, lambda x, y, z, c: (x, y, z + (1 if c == 0 else -1), c))
             whole = lax.dynamic_update_slice(whole, behind[None], ((at - sign * step) % ZS, 0, 0))
-    return whole.reshape(-1, piece.shape[1])
+    return whole.reshape(-1, piece.shape[1]), first
 
 
-def scale_kernel(grads_ref, moment_ref, scaled_ref, copies_ref):
-    scaled = grads_ref[...] * (1.0 / (jnp.sqrt(moment_ref[...]) + 1e-08))
-    scaled_ref[...] = scaled
+def copies_kernel(value_ref, copies_ref):
     for i in range(XS * YL):
-        copies_ref[i] = scaled
+        copies_ref[i] = value_ref[...]
 
 
-def scale(grads, second_moment):
+def copies_of(value):
     return pl.pallas_call(
-        scale_kernel,
-        out_shape=(jax.ShapeDtypeStruct((256, 256), jnp.float32),
-                   jax.ShapeDtypeStruct((XS * YL, 256, 256), jnp.float32)),
-        in_specs=[VMEM, VMEM],
-        out_specs=(VMEM, VMEM),
+        copies_kernel,
+        out_shape=jax.ShapeDtypeStruct((XS * YL, 256, 256), jnp.float32),
+        in_specs=[VMEM],
+        out_specs=VMEM,
         compiler_params=PARAMS,
-        cost_estimate=pl.CostEstimate(flops=65536, bytes_accessed=2621440, transcendentals=256),
-    )(grads, second_moment.reshape(1, 256))
+        cost_estimate=pl.CostEstimate(flops=0, bytes_accessed=2359296, transcendentals=0),
+    )(value)
 
 
 def halves(value):
@@ -173,11 +171,13 @@
     z, y_lo = ex % ZS, ex // ZS
     x, y_hi, core = feat // (YH * CS), (feat // CS) % YH, feat % CS
 
-    scaled, copies = scale(grads, second_moment)
+    scaled = grads * (1.0 / (jnp.sqrt(second_moment) + 1e-08))[None, :]
+    copies = copies_of(scaled)
     swapped = lax.all_to_all(scaled.reshape(XS, 64, 256), "feat", 0, 0, axis_index_groups=X_GROUPS, tiled=True)
     piece = jnp.transpose(swapped, (1, 0, 2)).reshape(64, XS * 256)
+    right, first = ring(piece, z, 1 - 2 * core)
+    copies, _ = lax.optimization_barrier((copies, first))
     left = lax.all_to_all(copies, AXES, 0, 0, axis_index_groups=LEFT_GROUPS, tiled=True)
-    right = ring(piece, z, 1 - 2 * core)
 
     mine, theirs = product(core, left, right)
     mine = mine + shift(theirs, lambda x, y, z, c: (x, y, z, c + 1))

time: 107 us -> 110 us (1.028)
  waiting for transfers between devices: 34.7 us -> 37.4 us
  other arithmetic: 0.99 us -> 2.65 us
  local copies, waits for them, and re-layouts: 2.38 us -> 0.75 us
    all_to_all x1, starting transfers between devices: 8.34 us -> 4.67 us  [shards(): lax.all_to_all(copies, AXES, 0, 0, axis_index_groups=LEFT_GROUPS, tiled=T...]
    ppermute x8, starting transfers between devices: 31.7 us -> 35.4 us  [shift(): return lax.ppermute(value, AXES, pairs)]
    ppermute x8, waiting for transfers between devices: 14.3 us -> 16.9 us  [shift(): return lax.ppermute(value, AXES, pairs)]
    unnamed x4 -> x0, local copies, waits for them, and re-layouts: 1.63 us -> none
  transfers between devices with their start and end apart: 10 -> 10, of which waited for: 8 -> 8; matrix products, arithmetic and copies ran while one was open for 1% -> 1% of each run, Pallas kernels for 0% -> 1%
where the time goes in v4:
time: 110 us; the launch traced here: 109 us
  starting transfers between devices  50.3 us (46%)
  waiting for transfers between devices  37.4 us (34%)
  blocking collectives  10.8 us (10%)
  Pallas kernels  6.94 us (6%)
  other arithmetic  2.65 us (2%)
    ppermute x8, starting transfers between devices, shift(): return lax.ppermute(value, AXES, pairs)  35.4 us
    all_to_all x1, waiting for transfers between devices, shards(): lax.all_to_all(mine, AXES, 0, 0, axis_index_groups=XY_GROUPS, tiled=True)  20.5 us
    ppermute x8, waiting for transfers between devices, shift(): return lax.ppermute(value, AXES, pairs)  16.9 us
    all_to_all x1, blocking collectives, shards(): lax.all_to_all(scaled.reshape(XS, 64, 256), 'feat', 0, 0, axis_index_grou...  10.8 us
    all_to_all x1, starting transfers between devices, shards(): lax.all_to_all(mine, AXES, 0, 0, axis_index_groups=XY_GROUPS, tiled=True)  10.2 us
    all_to_all x1, starting transfers between devices, shards(): lax.all_to_all(copies, AXES, 0, 0, axis_index_groups=LEFT_GROUPS, tiled=T...  4.67 us
    pallas_call x1, Pallas kernels, product(): pl.pallas_call(product_kernel, out_shape=(message, message), in_specs=[SM...  4.09 us
  transfers between devices with their start and end apart: 10, of which 8 were waited for; matrix products, arithmetic and copies ran while one was open for 1% of the time, Pallas kernels for 1%

profile of v4, /device:TPU:8, one launch (start us, length us, event | category | flops | bytes accessed | tf_op | source)
XLA Modules:
  0.0 109.2 jit_solution(15525505873570646487)
XLA Ops:
  0.0 0.7 add_divide_fusion
  0.7 1.0 broadcast_multiply_fusion.value_ref
  1.7 10.8 %all_to_all.15 = f32[4,64,256]{2,1,0:T(8,128)S(1)} all-to-all(f32[4,64,256]{2,1,0:T(8,128)S(1)} %bitcast.24), channel_id=1, replica_groups={{0,8,16,24},{1,9,17,25},{2,10,18,26},{3,11,19,27},{4,12,20,28},{5,13,21..., dimensions={0} | all-to-all | bytes 524288 | tf_op jit(solution)/shard_map/all_to_all | solution.py:176
  12.5 10.9 %collective-permute-start = (f32[64,1024]{1,0:T(8,128)S(1)}, f32[64,1024]{1,0:T(8,128)S(1)}, u32[]{:S(2)}, u32[]{:S(2)}) collective-permute-start(f32[64,1024]{1,0:T(8,128)S(1)} %bitcast.28), channel_id=1, source_target_pairs={{0,224},{1,33},{32,0},{33,65},{64,32},{65,97},{96,64},{97,129},{12... | collective-permute-start | bytes 786440 | tf_op jit(solution)/shard_map/ppermute | solution.py:36
  23.4 1.4 %shard_map.28 = f32[8,256,256]{2,1,0:T(8,128)} custom-call(f32[256,256]{1,0:T(8,128)S(1)} %broadcast_multiply_fusion.value_ref), custom_call_target="tpu_custom_call" | custom-call | bytes 2359296 | tf_op jit(solution)/shard_map/pallas_call | solution.py:58
  24.9 2.4 %collective-permute-done = f32[64,1024]{1,0:T(8,128)S(1)} collective-permute-done((f32[64,1024]{1,0:T(8,128)S(1)}, f32[64,1024]{1,0:T(8,128)S(1)}, u32[]{:S(2)}, u32[]{:S(2)}) %collective-permute-start) | collective-permute-done | bytes 262176 | tf_op jit(solution)/shard_map/ppermute | solution.py:36
  27.3 4.7 %all-to-all-start.1 = ((f32[8,256,256]{2,1,0:T(8,128)}), f32[8,256,256]{2,1,0:T(8,128)}, u32[]{:S(2)}, u32[]{:S(2)}) async-start(f32[8,256,256]{2,1,0:T(8,128)} %shard_map.28), calls=%async_computation.1 | async-start | bytes 4194304 | tf_op jit(solution)/shard_map/all_to_all | solution.py:180
  32.0 1.9 %collective-permute-start.1 = (f32[64,1024]{1,0:T(8,128)S(1)}, f32[64,1024]{1,0:T(8,128)S(1)}, u32[]{:S(2)}, u32[]{:S(2)}) collective-permute-start(f32[64,1024]{1,0:T(8,128)S(1)} %bitcast.29), channel_id=1, source_target_pairs={{0,32},{1,225},{32,64},{33,1},{64,96},{65,33},{96,128},{97,65},{12... | collective-permute-start | bytes 786440 | tf_op jit(solution)/shard_map/ppermute | solution.py:36
  34.7 5.6 %collective-permute-start.2 = (f32[64,1024]{1,0:T(8,128)S(1)}, f32[64,1024]{1,0:T(8,128)S(1)}, u32[]{:S(2)}, u32[]{:S(2)}) collective-permute-start(f32[64,1024]{1,0:T(8,128)S(1)} %collective-permute-done), channel_id=1, source_target_pairs={{0,224},{1,33},{32,0},{33,65},{64,32},{65,97},{96,64},{97,129},{12... | collective-permute-start | bytes 786440 | tf_op jit(solution)/shard_map/ppermute | solution.py:36
  40.3 4.0 %collective-permute-done.1 = f32[64,1024]{1,0:T(8,128)S(1)} collective-permute-done((f32[64,1024]{1,0:T(8,128)S(1)}, f32[64,1024]{1,0:T(8,128)S(1)}, u32[]{:S(2)}, u32[]{:S(2)}) %collective-permute-start.1) | collective-permute-done | bytes 262176 | tf_op jit(solution)/shard_map/ppermute | solution.py:36
  44.3 1.9 %collective-permute-start.3 = (f32[64,1024]{1,0:T(8,128)S(1)}, f32[64,1024]{1,0:T(8,128)S(1)}, u32[]{:S(2)}, u32[]{:S(2)}) collective-permute-start(f32[64,1024]{1,0:T(8,128)S(1)} %collective-permute-done.1), channel_id=1, source_target_pairs={{0,32},{1,225},{32,64},{33,1},{64,96},{65,33},{96,128},{97,65},{12... | collective-permute-start | bytes 786440 | tf_op jit(solution)/shard_map/ppermute | solution.py:36
  46.3 5.6 %collective-permute-start.4 = (f32[64,1024]{1,0:T(8,128)S(1)}, f32[64,1024]{1,0:T(8,128)S(1)}, u32[]{:S(2)}, u32[]{:S(2)}) collective-permute-start(f32[64,1024]{1,0:T(8,128)S(1)} %collective-permute-done.2), channel_id=1, source_target_pairs={{0,224},{1,33},{32,0},{33,65},{64,32},{65,97},{96,64},{97,129},{12... | collective-permute-start | bytes 786440 | tf_op jit(solution)/shard_map/ppermute | solution.py:36
  51.9 4.3 %collective-permute-done.3 = f32[64,1024]{1,0:T(8,128)S(1)} collective-permute-done((f32[64,1024]{1,0:T(8,128)S(1)}, f32[64,1024]{1,0:T(8,128)S(1)}, u32[]{:S(2)}, u32[]{:S(2)}) %collective-permute-start.3) | collective-permute-done | bytes 262176 | tf_op jit(solution)/shard_map/ppermute | solution.py:36
  56.2 1.9 %collective-permute-start.5 = (f32[64,1024]{1,0:T(8,128)S(1)}, f32[64,1024]{1,0:T(8,128)S(1)}, u32[]{:S(2)}, u32[]{:S(2)}) collective-permute-start(f32[64,1024]{1,0:T(8,128)S(1)} %collective-permute-done.3), channel_id=1, source_target_pairs={{0,32},{1,225},{32,64},{33,1},{64,96},{65,33},{96,128},{97,65},{12... | collective-permute-start | bytes 786440 | tf_op jit(solution)/shard_map/ppermute | solution.py:36
  58.5 5.6 %collective-permute-start.6 = (f32[64,1024]{1,0:T(8,128)S(1)}, f32[64,1024]{1,0:T(8,128)S(1)}, u32[]{:S(2)}, u32[]{:S(2)}) collective-permute-start(f32[64,1024]{1,0:T(8,128)S(1)} %collective-permute-done.4), channel_id=1, source_target_pairs={{0,224},{1,33},{32,0},{33,65},{64,32},{65,97},{96,64},{97,129},{12... | collective-permute-start | bytes 786440 | tf_op jit(solution)/shard_map/ppermute | solution.py:36
  64.1 3.4 %collective-permute-done.5 = f32[64,1024]{1,0:T(8,128)S(1)} collective-permute-done((f32[64,1024]{1,0:T(8,128)S(1)}, f32[64,1024]{1,0:T(8,128)S(1)}, u32[]{:S(2)}, u32[]{:S(2)}) %collective-permute-start.5) | collective-permute-done | bytes 262176 | tf_op jit(solution)/shard_map/ppermute | solution.py:36
  67.5 0.4 collective-permute-done.6
  68.0 4.1 %shard_map.29 = (f32[32,5,8,128]{3,2,1,0:T(8,128)S(1)}, f32[32,5,8,128]{3,2,1,0:T(8,128)S(1)}) custom-call(s32[1]{0:T(128)} %bitcast.4.core_ref, f32[8,256,256]{2,1,0:T(8,128)} %all-to-all-done.1.left_ref, f32[512,1024]{1,0:T(8,128)S(1)} %bitcast.25), custom_call_target="tpu_custom_call" | custom-call | flops 1610612736 | bytes 5505024 | tf_op jit(solution)/shard_map/pallas_call | solution.py:119
  72.1 1.9 %collective-permute-start.7 = (f32[32,5,8,128]{3,2,1,0:T(8,128)S(1)}, f32[32,5,8,128]{3,2,1,0:T(8,128)S(1)}, u32[]{:S(2)}, u32[]{:S(2)}) collective-permute-start(f32[32,5,8,128]{3,2,1,0:T(8,128)S(1)} %get-tuple-element.10), channel_id=1, source_target_pairs={{0,1},{1,0},{32,33},{33,32},{64,65},{65,64},{96,97},{97,96},{128,1... | collective-permute-start | bytes 1966088 | tf_op jit(solution)/shard_map/ppermute | solution.py:36
  74.0 2.1 %collective-permute-done.7 = f32[32,5,8,128]{3,2,1,0:T(8,128)S(1)} collective-permute-done((f32[32,5,8,128]{3,2,1,0:T(8,128)S(1)}, f32[32,5,8,128]{3,2,1,0:T(8,128)S(1)}, u32[]{:S(2)}, u32[]{:S(2)}) %collective-permute-start.7) | collective-permute-done | bytes 655392 | tf_op jit(solution)/shard_map/ppermute | solution.py:36
  76.1 0.9 add.107
  77.0 10.2 %all-to-all-start.2 = ((f32[32,5,8,128]{3,2,1,0:T(8,128)}), f32[32,5,8,128]{3,2,1,0:T(8,128)S(1)}, u32[]{:S(2)}, u32[]{:S(2)}) async-start(f32[32,5,8,128]{3,2,1,0:T(8,128)} %add.107), calls=%async_computation.2 | async-start | bytes 1310720 | tf_op jit(solution)/shard_map/all_to_all | solution.py:184
  87.4 20.5 %all-to-all-done.2.whole_ref = f32[32,5,8,128]{3,2,1,0:T(8,128)S(1)} async-done(((f32[32,5,8,128]{3,2,1,0:T(8,128)}), f32[32,5,8,128]{3,2,1,0:T(8,128)S(1)}, u32[]{:S(2)}, u32[]{:S(2)}) %all-to-all-start.2) | async-done | bytes 655392 | tf_op jit(solution)/shard_map/all_to_all | solution.py:184
  107.8 1.4 %shard_map.30 = f32[8,4096]{1,0:T(8,128)} custom-call(s32[4]{0:T(128)S(1)} %pad_add_fusion.place_ref, f32[32,5,8,128]{3,2,1,0:T(8,128)S(1)} %all-to-all-done.2.whole_ref), custom_call_target="tpu_custom_call" | custom-call | flops 262144 | bytes 786432 | tf_op jit(solution)/shard_map/pallas_call | solution.py:158
  (16 shorter events, 1.1 us)
Async XLA Ops:
  12.5 14.8 %collective-permute-start = (f32[64,1024]{1,0:T(8,128)S(1)}, f32[64,1024]{1,0:T(8,128)S(1)}, u32[]{:S(2)}, u32[]{:S(2)}) collective-permute-start(f32[64,1024]{1,0:T(8,128)S(1)} %bitcast.28), channel_id=1, source_target_pairs={{0,224},{1,33},{32,0},{33,65},{64,32},{65,97},{96,64},{97,129},{12... | collective-permute-start | bytes 786440 | tf_op jit(solution)/shard_map/ppermute | solution.py:36
  27.3 40.7 %all-to-all-start.1 = ((f32[8,256,256]{2,1,0:T(8,128)}), f32[8,256,256]{2,1,0:T(8,128)}, u32[]{:S(2)}, u32[]{:S(2)}) async-start(f32[8,256,256]{2,1,0:T(8,128)} %shard_map.28), calls=%async_computation.1 | async-start | bytes 4194304 | tf_op jit(solution)/shard_map/all_to_all | solution.py:180
  32.0 12.4 %collective-permute-start.1 = (f32[64,1024]{1,0:T(8,128)S(1)}, f32[64,1024]{1,0:T(8,128)S(1)}, u32[]{:S(2)}, u32[]{:S(2)}) collective-permute-start(f32[64,1024]{1,0:T(8,128)S(1)} %bitcast.29), channel_id=1, source_target_pairs={{0,32},{1,225},{32,64},{33,1},{64,96},{65,33},{96,128},{97,65},{12... | collective-permute-start | bytes 786440 | tf_op jit(solution)/shard_map/ppermute | solution.py:36
  34.7 11.7 %collective-permute-start.2 = (f32[64,1024]{1,0:T(8,128)S(1)}, f32[64,1024]{1,0:T(8,128)S(1)}, u32[]{:S(2)}, u32[]{:S(2)}) collective-permute-start(f32[64,1024]{1,0:T(8,128)S(1)} %collective-permute-done), channel_id=1, source_target_pairs={{0,224},{1,33},{32,0},{33,65},{64,32},{65,97},{96,64},{97,129},{12... | collective-permute-start | bytes 786440 | tf_op jit(solution)/shard_map/ppermute | solution.py:36
  44.3 11.9 %collective-permute-start.3 = (f32[64,1024]{1,0:T(8,128)S(1)}, f32[64,1024]{1,0:T(8,128)S(1)}, u32[]{:S(2)}, u32[]{:S(2)}) collective-permute-start(f32[64,1024]{1,0:T(8,128)S(1)} %collective-permute-done.1), channel_id=1, source_target_pairs={{0,32},{1,225},{32,64},{33,1},{64,96},{65,33},{96,128},{97,65},{12... | collective-permute-start | bytes 786440 | tf_op jit(solution)/shard_map/ppermute | solution.py:36
  46.3 12.2 %collective-permute-start.4 = (f32[64,1024]{1,0:T(8,128)S(1)}, f32[64,1024]{1,0:T(8,128)S(1)}, u32[]{:S(2)}, u32[]{:S(2)}) collective-permute-start(f32[64,1024]{1,0:T(8,128)S(1)} %collective-permute-done.2), channel_id=1, source_target_pairs={{0,224},{1,33},{32,0},{33,65},{64,32},{65,97},{96,64},{97,129},{12... | collective-permute-start | bytes 786440 | tf_op jit(solution)/shard_map/ppermute | solution.py:36
  56.2 11.3 %collective-permute-start.5 = (f32[64,1024]{1,0:T(8,128)S(1)}, f32[64,1024]{1,0:T(8,128)S(1)}, u32[]{:S(2)}, u32[]{:S(2)}) collective-permute-start(f32[64,1024]{1,0:T(8,128)S(1)} %collective-permute-done.3), channel_id=1, source_target_pairs={{0,32},{1,225},{32,64},{33,1},{64,96},{65,33},{96,128},{97,65},{12... | collective-permute-start | bytes 786440 | tf_op jit(solution)/shard_map/ppermute | solution.py:36
  58.5 9.5 %collective-permute-start.6 = (f32[64,1024]{1,0:T(8,128)S(1)}, f32[64,1024]{1,0:T(8,128)S(1)}, u32[]{:S(2)}, u32[]{:S(2)}) collective-permute-start(f32[64,1024]{1,0:T(8,128)S(1)} %collective-permute-done.4), channel_id=1, source_target_pairs={{0,224},{1,33},{32,0},{33,65},{64,32},{65,97},{96,64},{97,129},{12... | collective-permute-start | bytes 786440 | tf_op jit(solution)/shard_map/ppermute | solution.py:36
  72.1 4.0 %collective-permute-start.7 = (f32[32,5,8,128]{3,2,1,0:T(8,128)S(1)}, f32[32,5,8,128]{3,2,1,0:T(8,128)S(1)}, u32[]{:S(2)}, u32[]{:S(2)}) collective-permute-start(f32[32,5,8,128]{3,2,1,0:T(8,128)S(1)} %get-tuple-element.10), channel_id=1, source_target_pairs={{0,1},{1,0},{32,33},{33,32},{64,65},{65,64},{96,97},{97,96},{128,1... | collective-permute-start | bytes 1966088 | tf_op jit(solution)/shard_map/ppermute | solution.py:36
  77.0 30.9 %all-to-all-start.2 = ((f32[32,5,8,128]{3,2,1,0:T(8,128)}), f32[32,5,8,128]{3,2,1,0:T(8,128)S(1)}, u32[]{:S(2)}, u32[]{:S(2)}) async-start(f32[32,5,8,128]{3,2,1,0:T(8,128)} %add.107), calls=%async_computation.2 | async-start | bytes 1310720 | tf_op jit(solution)/shard_map/all_to_all | solution.py:184

commit v5 on v4

--- a/solution.py
+++ b/solution.py
@@ -41,10 +41,10 @@
     ahead, behind = piece, piece
     for step in range(1, 5):
         ahead = shift(ahead, lambda x, y, z, c: (x, y, z + (-1 if c == 0 else 1), c))
-        first = ahead if step == 1 else first
         whole = lax.dynamic_update_slice(whole, ahead[None], ((at + sign * step) % ZS, 0, 0))
         if step < 4:
             behind = shift(behind, lambda x, y, z, c: (x, y, z + (1 if c == 0 else -1), c))
+            first = behind if step == 1 else first
             whole = lax.dynamic_update_slice(whole, behind[None], ((at - sign * step) % ZS, 0, 0))
     return whole.reshape(-1, piece.shape[1]), first
 

time: 110 us -> 113 us (1.027)
  waiting for transfers between devices: 37.4 us -> 45.8 us
  starting transfers between devices: 50.3 us -> 45.6 us
    ppermute x8, waiting for transfers between devices: 16.9 us -> 25.3 us  [shift(): return lax.ppermute(value, AXES, pairs)]
    ppermute x8, starting transfers between devices: 35.4 us -> 30.7 us  [shift(): return lax.ppermute(value, AXES, pairs)]
where the time goes in v5:
time: 113 us
  waiting for transfers between devices  45.8 us (41%)
  starting transfers between devices  45.6 us (40%)
  blocking collectives  10.8 us (10%)
  Pallas kernels  6.94 us (6%)
  other arithmetic  2.65 us (2%)
    ppermute x8, starting transfers between devices, shift(): return lax.ppermute(value, AXES, pairs)  30.7 us
    ppermute x8, waiting for transfers between devices, shift(): return lax.ppermute(value, AXES, pairs)  25.3 us
    all_to_all x1, waiting for transfers between devices, shards(): lax.all_to_all(mine, AXES, 0, 0, axis_index_groups=XY_GROUPS, tiled=True)  20.5 us
    all_to_all x1, blocking collectives, shards(): lax.all_to_all(scaled.reshape(XS, 64, 256), 'feat', 0, 0, axis_index_grou...  10.8 us
    all_to_all x1, starting transfers between devices, shards(): lax.all_to_all(mine, AXES, 0, 0, axis_index_groups=XY_GROUPS, tiled=True)  10.3 us
    all_to_all x1, starting transfers between devices, shards(): lax.all_to_all(copies, AXES, 0, 0, axis_index_groups=LEFT_GROUPS, tiled=T...  4.67 us
    pallas_call x1, Pallas kernels, product(): pl.pallas_call(product_kernel, out_shape=(message, message), in_specs=[SM...  4.09 us
  transfers between devices with their start and end apart: 10, of which 8 were waited for; matrix products, arithmetic and copies ran while one was open for 1% of the time, Pallas kernels for 1%

profile of v5, /device:TPU:8, one launch (start us, length us, event | category | flops | bytes accessed | tf_op | source)
XLA Modules:
  0.0 112.9 jit_solution(10351320993895551878)
XLA Ops:
  0.7 1.0 broadcast_multiply_fusion.value_ref
  1.7 10.8 %all_to_all.15 = f32[4,64,256]{2,1,0:T(8,128)S(1)} all-to-all(f32[4,64,256]{2,1,0:T(8,128)S(1)} %bitcast.24), channel_id=1, replica_groups={{0,8,16,24},{1,9,17,25},{2,10,18,26},{3,11,19,27},{4,12,20,28},{5,13,21..., dimensions={0} | all-to-all | bytes 524288 | tf_op jit(solution)/shard_map/all_to_all | solution.py:176
  12.5 4.3 %collective-permute-start = (f32[64,1024]{1,0:T(8,128)S(1)}, f32[64,1024]{1,0:T(8,128)S(1)}, u32[]{:S(2)}, u32[]{:S(2)}) collective-permute-start(f32[64,1024]{1,0:T(8,128)S(1)} %bitcast.28), channel_id=1, source_target_pairs={{0,32},{1,225},{32,64},{33,1},{64,96},{65,33},{96,128},{97,65},{12... | collective-permute-start | bytes 786440 | tf_op jit(solution)/shard_map/ppermute | solution.py:36
  16.8 1.4 %shard_map.28 = f32[8,256,256]{2,1,0:T(8,128)} custom-call(f32[256,256]{1,0:T(8,128)S(1)} %broadcast_multiply_fusion.value_ref), custom_call_target="tpu_custom_call" | custom-call | bytes 2359296 | tf_op jit(solution)/shard_map/pallas_call | solution.py:58
  18.2 9.6 %collective-permute-done = f32[64,1024]{1,0:T(8,128)S(1)} collective-permute-done((f32[64,1024]{1,0:T(8,128)S(1)}, f32[64,1024]{1,0:T(8,128)S(1)}, u32[]{:S(2)}, u32[]{:S(2)}) %collective-permute-start) | collective-permute-done | bytes 262176 | tf_op jit(solution)/shard_map/ppermute | solution.py:36
  27.8 4.7 %all-to-all-start.1 = ((f32[8,256,256]{2,1,0:T(8,128)}), f32[8,256,256]{2,1,0:T(8,128)}, u32[]{:S(2)}, u32[]{:S(2)}) async-start(f32[8,256,256]{2,1,0:T(8,128)} %shard_map.28), calls=%async_computation.1 | async-start | bytes 4194304 | tf_op jit(solution)/shard_map/all_to_all | solution.py:180
  32.4 3.9 %collective-permute-start.1 = (f32[64,1024]{1,0:T(8,128)S(1)}, f32[64,1024]{1,0:T(8,128)S(1)}, u32[]{:S(2)}, u32[]{:S(2)}) collective-permute-start(f32[64,1024]{1,0:T(8,128)S(1)} %bitcast.29), channel_id=1, source_target_pairs={{0,224},{1,33},{32,0},{33,65},{64,32},{65,97},{96,64},{97,129},{12... | collective-permute-start | bytes 786440 | tf_op jit(solution)/shard_map/ppermute | solution.py:36
  37.1 1.9 %collective-permute-start.3 = (f32[64,1024]{1,0:T(8,128)S(1)}, f32[64,1024]{1,0:T(8,128)S(1)}, u32[]{:S(2)}, u32[]{:S(2)}) collective-permute-start(f32[64,1024]{1,0:T(8,128)S(1)} %collective-permute-done), channel_id=1, source_target_pairs={{0,32},{1,225},{32,64},{33,1},{64,96},{65,33},{96,128},{97,65},{12... | collective-permute-start | bytes 786440 | tf_op jit(solution)/shard_map/ppermute | solution.py:36
  39.1 4.0 %collective-permute-done.1 = f32[64,1024]{1,0:T(8,128)S(1)} collective-permute-done((f32[64,1024]{1,0:T(8,128)S(1)}, f32[64,1024]{1,0:T(8,128)S(1)}, u32[]{:S(2)}, u32[]{:S(2)}) %collective-permute-start.1) | collective-permute-done | bytes 262176 | tf_op jit(solution)/shard_map/ppermute | solution.py:36
  43.0 5.6 %collective-permute-start.2 = (f32[64,1024]{1,0:T(8,128)S(1)}, f32[64,1024]{1,0:T(8,128)S(1)}, u32[]{:S(2)}, u32[]{:S(2)}) collective-permute-start(f32[64,1024]{1,0:T(8,128)S(1)} %collective-permute-done.1), channel_id=1, source_target_pairs={{0,224},{1,33},{32,0},{33,65},{64,32},{65,97},{96,64},{97,129},{12... | collective-permute-start | bytes 786440 | tf_op jit(solution)/shard_map/ppermute | solution.py:36
  48.6 3.8 %collective-permute-done.2 = f32[64,1024]{1,0:T(8,128)S(1)} collective-permute-done((f32[64,1024]{1,0:T(8,128)S(1)}, f32[64,1024]{1,0:T(8,128)S(1)}, u32[]{:S(2)}, u32[]{:S(2)}) %collective-permute-start.2) | collective-permute-done | bytes 262176 | tf_op jit(solution)/shard_map/ppermute | solution.py:36
  52.4 5.6 %collective-permute-start.4 = (f32[64,1024]{1,0:T(8,128)S(1)}, f32[64,1024]{1,0:T(8,128)S(1)}, u32[]{:S(2)}, u32[]{:S(2)}) collective-permute-start(f32[64,1024]{1,0:T(8,128)S(1)} %collective-permute-done.2), channel_id=1, source_target_pairs={{0,224},{1,33},{32,0},{33,65},{64,32},{65,97},{96,64},{97,129},{12... | collective-permute-start | bytes 786440 | tf_op jit(solution)/shard_map/ppermute | solution.py:36
  58.0 1.9 %collective-permute-start.5 = (f32[64,1024]{1,0:T(8,128)S(1)}, f32[64,1024]{1,0:T(8,128)S(1)}, u32[]{:S(2)}, u32[]{:S(2)}) collective-permute-start(f32[64,1024]{1,0:T(8,128)S(1)} %collective-permute-done.3), channel_id=1, source_target_pairs={{0,32},{1,225},{32,64},{33,1},{64,96},{65,33},{96,128},{97,65},{12... | collective-permute-start | bytes 786440 | tf_op jit(solution)/shard_map/ppermute | solution.py:36
  60.0 2.1 %collective-permute-done.4 = f32[64,1024]{1,0:T(8,128)S(1)} collective-permute-done((f32[64,1024]{1,0:T(8,128)S(1)}, f32[64,1024]{1,0:T(8,128)S(1)}, u32[]{:S(2)}, u32[]{:S(2)}) %collective-permute-start.4) | collective-permute-done | bytes 262176 | tf_op jit(solution)/shard_map/ppermute | solution.py:36
  62.1 5.6 %collective-permute-start.6 = (f32[64,1024]{1,0:T(8,128)S(1)}, f32[64,1024]{1,0:T(8,128)S(1)}, u32[]{:S(2)}, u32[]{:S(2)}) collective-permute-start(f32[64,1024]{1,0:T(8,128)S(1)} %collective-permute-done.4), channel_id=1, source_target_pairs={{0,224},{1,33},{32,0},{33,65},{64,32},{65,97},{96,64},{97,129},{12... | collective-permute-start | bytes 786440 | tf_op jit(solution)/shard_map/ppermute | solution.py:36
  67.8 1.5 %collective-permute-done.5 = f32[64,1024]{1,0:T(8,128)S(1)} collective-permute-done((f32[64,1024]{1,0:T(8,128)S(1)}, f32[64,1024]{1,0:T(8,128)S(1)}, u32[]{:S(2)}, u32[]{:S(2)}) %collective-permute-start.5) | collective-permute-done | bytes 262176 | tf_op jit(solution)/shard_map/ppermute | solution.py:36
  69.3 2.3 %collective-permute-done.6 = f32[64,1024]{1,0:T(8,128)S(1)} collective-permute-done((f32[64,1024]{1,0:T(8,128)S(1)}, f32[64,1024]{1,0:T(8,128)S(1)}, u32[]{:S(2)}, u32[]{:S(2)}) %collective-permute-start.6) | collective-permute-done | bytes 262176 | tf_op jit(solution)/shard_map/ppermute | solution.py:36
  71.6 4.1 %shard_map.29 = (f32[32,5,8,128]{3,2,1,0:T(8,128)S(1)}, f32[32,5,8,128]{3,2,1,0:T(8,128)S(1)}) custom-call(s32[1]{0:T(128)} %bitcast.4.core_ref, f32[8,256,256]{2,1,0:T(8,128)} %all-to-all-done.1.left_ref, f32[512,1024]{1,0:T(8,128)S(1)} %bitcast.25), custom_call_target="tpu_custom_call" | custom-call | flops 1610612736 | bytes 5505024 | tf_op jit(solution)/shard_map/pallas_call | solution.py:119
  75.7 1.9 %collective-permute-start.7 = (f32[32,5,8,128]{3,2,1,0:T(8,128)S(1)}, f32[32,5,8,128]{3,2,1,0:T(8,128)S(1)}, u32[]{:S(2)}, u32[]{:S(2)}) collective-permute-start(f32[32,5,8,128]{3,2,1,0:T(8,128)S(1)} %get-tuple-element.10), channel_id=1, source_target_pairs={{0,1},{1,0},{32,33},{33,32},{64,65},{65,64},{96,97},{97,96},{128,1... | collective-permute-start | bytes 1966088 | tf_op jit(solution)/shard_map/ppermute | solution.py:36
  77.7 2.1 %collective-permute-done.7 = f32[32,5,8,128]{3,2,1,0:T(8,128)S(1)} collective-permute-done((f32[32,5,8,128]{3,2,1,0:T(8,128)S(1)}, f32[32,5,8,128]{3,2,1,0:T(8,128)S(1)}, u32[]{:S(2)}, u32[]{:S(2)}) %collective-permute-start.7) | collective-permute-done | bytes 655392 | tf_op jit(solution)/shard_map/ppermute | solution.py:36
  79.7 0.9 add.107
  80.6 10.3 %all-to-all-start.2 = ((f32[32,5,8,128]{3,2,1,0:T(8,128)}), f32[32,5,8,128]{3,2,1,0:T(8,128)S(1)}, u32[]{:S(2)}, u32[]{:S(2)}) async-start(f32[32,5,8,128]{3,2,1,0:T(8,128)} %add.107), calls=%async_computation.2 | async-start | bytes 1310720 | tf_op jit(solution)/shard_map/all_to_all | solution.py:184
  91.0 20.5 %all-to-all-done.2.whole_ref = f32[32,5,8,128]{3,2,1,0:T(8,128)S(1)} async-done(((f32[32,5,8,128]{3,2,1,0:T(8,128)}), f32[32,5,8,128]{3,2,1,0:T(8,128)S(1)}, u32[]{:S(2)}, u32[]{:S(2)}) %all-to-all-start.2) | async-done | bytes 655392 | tf_op jit(solution)/shard_map/all_to_all | solution.py:184
  111.5 1.4 %shard_map.30 = f32[8,4096]{1,0:T(8,128)} custom-call(s32[4]{0:T(128)S(1)} %pad_add_fusion.place_ref, f32[32,5,8,128]{3,2,1,0:T(8,128)S(1)} %all-to-all-done.2.whole_ref), custom_call_target="tpu_custom_call" | custom-call | flops 262144 | bytes 786432 | tf_op jit(solution)/shard_map/pallas_call | solution.py:158
  (16 shorter events, 1.5 us)
Async XLA Ops:
  12.5 15.3 %collective-permute-start = (f32[64,1024]{1,0:T(8,128)S(1)}, f32[64,1024]{1,0:T(8,128)S(1)}, u32[]{:S(2)}, u32[]{:S(2)}) collective-permute-start(f32[64,1024]{1,0:T(8,128)S(1)} %bitcast.28), channel_id=1, source_target_pairs={{0,32},{1,225},{32,64},{33,1},{64,96},{65,33},{96,128},{97,65},{12... | collective-permute-start | bytes 786440 | tf_op jit(solution)/shard_map/ppermute | solution.py:36
  27.8 43.9 %all-to-all-start.1 = ((f32[8,256,256]{2,1,0:T(8,128)}), f32[8,256,256]{2,1,0:T(8,128)}, u32[]{:S(2)}, u32[]{:S(2)}) async-start(f32[8,256,256]{2,1,0:T(8,128)} %shard_map.28), calls=%async_computation.1 | async-start | bytes 4194304 | tf_op jit(solution)/shard_map/all_to_all | solution.py:180
  32.4 10.6 %collective-permute-start.1 = (f32[64,1024]{1,0:T(8,128)S(1)}, f32[64,1024]{1,0:T(8,128)S(1)}, u32[]{:S(2)}, u32[]{:S(2)}) collective-permute-start(f32[64,1024]{1,0:T(8,128)S(1)} %bitcast.29), channel_id=1, source_target_pairs={{0,224},{1,33},{32,0},{33,65},{64,32},{65,97},{96,64},{97,129},{12... | collective-permute-start | bytes 786440 | tf_op jit(solution)/shard_map/ppermute | solution.py:36
  37.1 20.9 %collective-permute-start.3 = (f32[64,1024]{1,0:T(8,128)S(1)}, f32[64,1024]{1,0:T(8,128)S(1)}, u32[]{:S(2)}, u32[]{:S(2)}) collective-permute-start(f32[64,1024]{1,0:T(8,128)S(1)} %collective-permute-done), channel_id=1, source_target_pairs={{0,32},{1,225},{32,64},{33,1},{64,96},{65,33},{96,128},{97,65},{12... | collective-permute-start | bytes 786440 | tf_op jit(solution)/shard_map/ppermute | solution.py:36
  43.0 9.4 %collective-permute-start.2 = (f32[64,1024]{1,0:T(8,128)S(1)}, f32[64,1024]{1,0:T(8,128)S(1)}, u32[]{:S(2)}, u32[]{:S(2)}) collective-permute-start(f32[64,1024]{1,0:T(8,128)S(1)} %collective-permute-done.1), channel_id=1, source_target_pairs={{0,224},{1,33},{32,0},{33,65},{64,32},{65,97},{96,64},{97,129},{12... | collective-permute-start | bytes 786440 | tf_op jit(solution)/shard_map/ppermute | solution.py:36
  52.4 9.7 %collective-permute-start.4 = (f32[64,1024]{1,0:T(8,128)S(1)}, f32[64,1024]{1,0:T(8,128)S(1)}, u32[]{:S(2)}, u32[]{:S(2)}) collective-permute-start(f32[64,1024]{1,0:T(8,128)S(1)} %collective-permute-done.2), channel_id=1, source_target_pairs={{0,224},{1,33},{32,0},{33,65},{64,32},{65,97},{96,64},{97,129},{12... | collective-permute-start | bytes 786440 | tf_op jit(solution)/shard_map/ppermute | solution.py:36
  58.0 11.2 %collective-permute-start.5 = (f32[64,1024]{1,0:T(8,128)S(1)}, f32[64,1024]{1,0:T(8,128)S(1)}, u32[]{:S(2)}, u32[]{:S(2)}) collective-permute-start(f32[64,1024]{1,0:T(8,128)S(1)} %collective-permute-done.3), channel_id=1, source_target_pairs={{0,32},{1,225},{32,64},{33,1},{64,96},{65,33},{96,128},{97,65},{12... | collective-permute-start | bytes 786440 | tf_op jit(solution)/shard_map/ppermute | solution.py:36
  62.1 9.5 %collective-permute-start.6 = (f32[64,1024]{1,0:T(8,128)S(1)}, f32[64,1024]{1,0:T(8,128)S(1)}, u32[]{:S(2)}, u32[]{:S(2)}) collective-permute-start(f32[64,1024]{1,0:T(8,128)S(1)} %collective-permute-done.4), channel_id=1, source_target_pairs={{0,224},{1,33},{32,0},{33,65},{64,32},{65,97},{96,64},{97,129},{12... | collective-permute-start | bytes 786440 | tf_op jit(solution)/shard_map/ppermute | solution.py:36
  75.7 4.0 %collective-permute-start.7 = (f32[32,5,8,128]{3,2,1,0:T(8,128)S(1)}, f32[32,5,8,128]{3,2,1,0:T(8,128)S(1)}, u32[]{:S(2)}, u32[]{:S(2)}) collective-permute-start(f32[32,5,8,128]{3,2,1,0:T(8,128)S(1)} %get-tuple-element.10), channel_id=1, source_target_pairs={{0,1},{1,0},{32,33},{33,32},{64,65},{65,64},{96,97},{97,96},{128,1... | collective-permute-start | bytes 1966088 | tf_op jit(solution)/shard_map/ppermute | solution.py:36
  80.6 30.9 %all-to-all-start.2 = ((f32[32,5,8,128]{3,2,1,0:T(8,128)}), f32[32,5,8,128]{3,2,1,0:T(8,128)S(1)}, u32[]{:S(2)}, u32[]{:S(2)}) async-start(f32[32,5,8,128]{3,2,1,0:T(8,128)} %add.107), calls=%async_computation.2 | async-start | bytes 1310720 | tf_op jit(solution)/shard_map/all_to_all | solution.py:184

commit v6 on v2

--- a/solution.py
+++ b/solution.py
@@ -1,3 +1,5 @@
+import functools
+
 import jax
 import jax.numpy as jnp
 from jax import lax
@@ -76,72 +78,73 @@
     return lax.dot_general(left, right, (((1,), (1,)), ((), ())), preferred_element_type=jnp.float32)
 
 
-def product_kernel(core_ref, left_ref, right_ref, mine_ref, theirs_ref, total_ref):
+def half_kernel(first, core_ref, left_ref, right_ref, *refs):
+    message_ref, tile_ref, total_ref = (refs[0], refs[1], refs[2]) if first else (refs[1], refs[0], refs[2])
+    core = core_ref[0]
     ones = jnp.ones((8, 256), jnp.bfloat16)
     sums = jnp.zeros((8, 512), jnp.float32)
     for x in range(XS):
         block = right_ref[:, x * 256:(x + 1) * 256]
         right_high, right_low = halves(block)
-        square_high, square_low = halves(block * block)
-        sums = sums + dot_t(ones, square_high) + dot_t(ones, square_low)
-        for yl in range(YL):
-            left_high, left_low = halves(left_ref[x * YL + yl])
-            part = dot_t(left_high, right_high) + dot_t(left_high, right_low) + dot_t(left_low, right_high)
-            if x == 0:
-                total_ref[yl] = part
-            else:
-                total_ref[yl] += part
-    row = lax.broadcasted_iota(jnp.int32, (8, 128), 0)
-    tile = jnp.zeros((8, 128), jnp.float32)
-    for q in range(4):
-        tile = jnp.where(row == q, sums[:, q * 128:(q + 1) * 128], tile)
-
-    def write(refs):
-        for x in range(XS):
-            for yh in range(YH):
-                for yl in range(YL):
-                    to = (x * YH + yh) * YL + yl
-                    for c in range(CS):
-                        at = x * 64 + yh * 16 + c * 8
-                        for q in range(4):
-                            refs[c][to, q] = total_ref[yl, at:at + 8, q * 128:(q + 1) * 128]
-                        refs[c][to, 4] = tile
-
-    @pl.when(core_ref[0] == 0)
-    def _():
-        write((mine_ref, theirs_ref))
-
-    @pl.when(core_ref[0] == 1)
-    def _():
-        write((theirs_ref, mine_ref))
+        if first:
+            square_high, square_low = halves(block * block)
+            sums = sums + dot_t(ones, square_high) + dot_t(ones, square_low)
+        rows = [left_ref[x * YL + yl, pl.ds(pl.multiple_of(i * 16 + core * 8, 8), 8), :]
+                for yl in range(YL) for i in range(XS * YH)]
+        left_high, left_low = halves(jnp.concatenate(rows, axis=0))
+        part = dot_t(left_high, right_high) + dot_t(left_high, right_low) + dot_t(left_low, right_high)
+        if x == 0:
+            total_ref[...] = part
+        else:
+            total_ref[...] += part
+    if first:
+        row = lax.broadcasted_iota(jnp.int32, (4, 128), 0)
+        tile = jnp.zeros((4, 128), jnp.float32)
+        for q in range(4):
+            tile = jnp.where(row == q, sums[:4, q * 128:(q + 1) * 128], tile)
+        tile_ref[...] = tile
+    else:
+        tile = tile_ref[...]
+    for yl in range(YL):
+        for i in range(XS * YH):
+            to = i * YL + yl
+            for q in range(4):
+                for half in range(2):
+                    top = (yl * XS * YH + i) * 8 + 4 * half
+                    message_ref[to, 2 * q + half] = total_ref[top:top + 4, q * 128:(q + 1) * 128]
+            message_ref[to, 8] = tile
 
 
-def product(core, left, right):
-    message = jax.ShapeDtypeStruct((XS * YS, 5, 8, 128), jnp.float32)
+def half_product(core, left, right, tile=None):
+    first = tile is None
+    message = jax.ShapeDtypeStruct((XS * YS, 9, 4, 128), jnp.float32)
+    sums = jax.ShapeDtypeStruct((4, 128), jnp.float32)
     return pl.pallas_call(
-        product_kernel,
-        out_shape=(message, message),
-        in_specs=[SMEM, VMEM, VMEM],
-        out_specs=(VMEM, VMEM),
-        scratch_shapes=[pltpu.VMEM((YL, 256, 512), jnp.float32)],
+        functools.partial(half_kernel, first),
+        out_shape=(message, sums) if first else message,
+        in_specs=[SMEM] + [VMEM] * (2 if first else 3),
+        out_specs=(VMEM, VMEM) if first else VMEM,
+        scratch_shapes=[pltpu.VMEM((256, 512), jnp.float32)],
         compiler_params=PARAMS,
-        cost_estimate=pl.CostEstimate(flops=3 * 2 * 512 * 512 * 1024, bytes_accessed=5505024, transcendentals=0),
-    )(core.reshape(1), left, right)
+        cost_estimate=pl.CostEstimate(flops=3 * 2 * 256 * 512 * 1024, bytes_accessed=4784128, transcendentals=0),
+    )(core.reshape(1), left, right, *(() if first else (tile,)))
 
 
 def finish_kernel(place_ref, whole_ref, out_ref, scale_ref):
     row = lax.broadcasted_iota(jnp.int32, (8, 128), 0)
+    part = lax.broadcasted_iota(jnp.int32, (4, 128), 0)
     lane = lax.broadcasted_iota(jnp.int32, (8, 128), 1)
     tiles = {}
     for x in range(XS):
         for yl in range(YL):
-            got = [sum(whole_ref[(x * YH + yh) * YL + yl, q] for yh in range(YH)) for q in range(5)]
-            factor = lax.rsqrt(got[4] + 1e-06)
+            got = [sum(whole_ref[(x * YH + yh) * YL + yl, q] for yh in range(YH)) for q in range(9)]
+            factor = lax.rsqrt(got[8] + 1e-06)
             scale_ref[x * YL + yl] = factor
             for q in range(4):
-                tiles[x, yl, q] = got[q] * factor[q:q + 1, :]
+                tile = jnp.concatenate([got[2 * q], got[2 * q + 1]], axis=0)
+                tiles[x, yl, q] = tile * factor[q:q + 1, :]
     x, yl, z, at = place_ref[0], place_ref[1], place_ref[2], place_ref[3]
-    own = jnp.where(row == z // 2, scale_ref[x * YL + yl], 0.0)
+    own = jnp.where(part == z // 2, scale_ref[x * YL + yl], 0.0)
     own = jnp.sum(own, axis=0, keepdims=True)
     own = jnp.where(lane == row + (z % 2) * 64 + at, own, 0.0)
     own = jnp.sum(own, axis=1, keepdims=True)
@@ -162,7 +165,7 @@
         out_shape=jax.ShapeDtypeStruct((8, 4096), jnp.float32),
         in_specs=[SMEM, VMEM],
         out_specs=VMEM,
-        scratch_shapes=[pltpu.VMEM((XS * YL, 8, 128), jnp.float32)],
+        scratch_shapes=[pltpu.VMEM((XS * YL, 4, 128), jnp.float32)],
         compiler_params=PARAMS,
         cost_estimate=pl.CostEstimate(flops=262144, bytes_accessed=786432, transcendentals=4096),
     )(place, whole)
@@ -179,8 +182,9 @@
     left = lax.all_to_all(copies, AXES, 0, 0, axis_index_groups=LEFT_GROUPS, tiled=True)
     right = ring(piece, z, 1 - 2 * core)
 
-    mine, theirs = product(core, left, right)
-    mine = mine + shift(theirs, lambda x, y, z, c: (x, y, z, c + 1))
+    theirs, tile = half_product(1 - core, left, right)
+    theirs = shift(theirs, lambda x, y, z, c: (x, y, z, c + 1))
+    mine = half_product(core, left, right, tile) + theirs
     whole = lax.all_to_all(mine, AXES, 0, 0, axis_index_groups=XY_GROUPS, tiled=True)
     return finish(jnp.stack([x, y_lo, z, y_hi * 16 + core * 8]), whole)
 

time: 107 us -> 105 us (0.981)
  local copies, waits for them, and re-layouts: 2.38 us -> 6.62 us
  waiting for transfers between devices: 34.7 us -> 31.9 us
  Pallas kernels: 6.99 us -> 4.39 us
    unnamed x4 -> x10, local copies, waits for them, and re-layouts: 1.63 us -> 5.86 us
    ppermute x8, waiting for transfers between devices: 14.3 us -> 12.7 us  [shift(): return lax.ppermute(value, AXES, pairs)]
    all_to_all x1, waiting for transfers between devices: 20.5 us -> 19.1 us  [shards(): lax.all_to_all(mine, AXES, 0, 0, axis_index_groups=XY_GROUPS, tiled=True)]
    pallas_call x1, Pallas kernels: 1.5 us -> 0.16 us  [scale(): pl.pallas_call(scale_kernel, out_shape=(jax.ShapeDtypeStruct((256, 256),...]
    pallas_call x1 -> x2, Pallas kernels: 4.09 us -> 2.82 us  [half_product(): pl.pallas_call(functools.partial(half_kernel, first), out_shape=(message,...]
  transfers between devices with their start and end apart: 10 -> 10, of which waited for: 8 -> 8; matrix products, arithmetic and copies ran while one was open for 1% -> 1% of each run, Pallas kernels for 0% -> 1%
where the time goes in v6:
time: 105 us
  starting transfers between devices  49.6 us (47%)
  waiting for transfers between devices  31.9 us (30%)
  blocking collectives  10.8 us (10%)
  local copies, waits for them, and re-layouts  6.62 us (6%)
  Pallas kernels  4.39 us (4%)
  other arithmetic  1.06 us (1%)
    ppermute x8, starting transfers between devices, shift(): return lax.ppermute(value, AXES, pairs)  31.7 us
    all_to_all x1, waiting for transfers between devices, shards(): lax.all_to_all(mine, AXES, 0, 0, axis_index_groups=XY_GROUPS, tiled=True)  19.1 us
    ppermute x8, waiting for transfers between devices, shift(): return lax.ppermute(value, AXES, pairs)  12.7 us
    all_to_all x1, blocking collectives, shards(): lax.all_to_all(scaled.reshape(XS, 64, 256), 'feat', 0, 0, axis_index_grou...  10.8 us
    all_to_all x1, starting transfers between devices, shards(): lax.all_to_all(mine, AXES, 0, 0, axis_index_groups=XY_GROUPS, tiled=True)  10.2 us
    all_to_all x1, starting transfers between devices, shards(): lax.all_to_all(copies, AXES, 0, 0, axis_index_groups=LEFT_GROUPS, tiled=T...  7.62 us
    unnamed x10, local copies, waits for them, and re-layouts  5.86 us
    pallas_call x2, Pallas kernels, half_product(): pl.pallas_call(functools.partial(half_kernel, first), out_shape=(message,...  2.82 us
  transfers between devices with their start and end apart: 10, of which 8 were waited for; matrix products, arithmetic and copies ran while one was open for 1% of the time, Pallas kernels for 1%

profile of v6, /device:TPU:8, one launch (start us, length us, event | category | flops | bytes accessed | tf_op | source)
XLA Modules:
  0.0 104.7 jit_solution(3152017113872419829)
XLA Ops:
  0.0 0.9 copy-done.3
  1.8 1.3 %copy-done.2 = f32[8,256,256]{2,1,0:T(8,128)} copy-done((f32[8,256,256]{2,1,0:T(8,128)}, f32[8,256,256]{2,1,0:T(8,128)S(1)}, u32[]{:S(2)}) %copy-start.2) | copy-done | bytes 2097176
  3.1 10.8 %all_to_all.15 = f32[4,64,256]{2,1,0:T(8,128)S(1)} all-to-all(f32[4,64,256]{2,1,0:T(8,128)S(1)} %bitcast.28), channel_id=1, replica_groups={{0,8,16,24},{1,9,17,25},{2,10,18,26},{3,11,19,27},{4,12,20,28},{5,13,21..., dimensions={0} | all-to-all | bytes 524288 | tf_op jit(solution)/shard_map/all_to_all | solution.py:180
  13.9 7.6 %all-to-all-start = ((f32[8,256,256]{2,1,0:T(8,128)}), f32[8,256,256]{2,1,0:T(8,128)S(1)}, u32[]{:S(2)}, u32[]{:S(2)}) async-start(f32[8,256,256]{2,1,0:T(8,128)} %copy-done.2), calls=%async_computation | async-start | bytes 4194304 | tf_op jit(solution)/shard_map/all_to_all | solution.py:182
  21.5 7.3 %collective-permute-start = (f32[64,1024]{1,0:T(8,128)S(1)}, f32[64,1024]{1,0:T(8,128)S(1)}, u32[]{:S(2)}, u32[]{:S(2)}) collective-permute-start(f32[64,1024]{1,0:T(8,128)S(1)} %bitcast.32), channel_id=1, source_target_pairs={{0,224},{1,33},{32,0},{33,65},{64,32},{65,97},{96,64},{97,129},{12... | collective-permute-start | bytes 786440 | tf_op jit(solution)/shard_map/ppermute | solution.py:38
  28.8 1.9 %collective-permute-start.1 = (f32[64,1024]{1,0:T(8,128)S(1)}, f32[64,1024]{1,0:T(8,128)S(1)}, u32[]{:S(2)}, u32[]{:S(2)}) collective-permute-start(f32[64,1024]{1,0:T(8,128)S(1)} %bitcast.33), channel_id=1, source_target_pairs={{0,32},{1,225},{32,64},{33,1},{64,96},{65,33},{96,128},{97,65},{12... | collective-permute-start | bytes 786440 | tf_op jit(solution)/shard_map/ppermute | solution.py:38
  31.5 3.1 %collective-permute-done = f32[64,1024]{1,0:T(8,128)S(1)} collective-permute-done((f32[64,1024]{1,0:T(8,128)S(1)}, f32[64,1024]{1,0:T(8,128)S(1)}, u32[]{:S(2)}, u32[]{:S(2)}) %collective-permute-start) | collective-permute-done | bytes 262176 | tf_op jit(solution)/shard_map/ppermute | solution.py:38
  34.6 5.6 %collective-permute-start.2 = (f32[64,1024]{1,0:T(8,128)S(1)}, f32[64,1024]{1,0:T(8,128)S(1)}, u32[]{:S(2)}, u32[]{:S(2)}) collective-permute-start(f32[64,1024]{1,0:T(8,128)S(1)} %collective-permute-done), channel_id=1, source_target_pairs={{0,224},{1,33},{32,0},{33,65},{64,32},{65,97},{96,64},{97,129},{12... | collective-permute-start | bytes 786440 | tf_op jit(solution)/shard_map/ppermute | solution.py:38
  40.2 1.9 %collective-permute-start.3 = (f32[64,1024]{1,0:T(8,128)S(1)}, f32[64,1024]{1,0:T(8,128)S(1)}, u32[]{:S(2)}, u32[]{:S(2)}) collective-permute-start(f32[64,1024]{1,0:T(8,128)S(1)} %collective-permute-done.1), channel_id=1, source_target_pairs={{0,32},{1,225},{32,64},{33,1},{64,96},{65,33},{96,128},{97,65},{12... | collective-permute-start | bytes 786440 | tf_op jit(solution)/shard_map/ppermute | solution.py:38
  42.2 2.9 %collective-permute-done.2 = f32[64,1024]{1,0:T(8,128)S(1)} collective-permute-done((f32[64,1024]{1,0:T(8,128)S(1)}, f32[64,1024]{1,0:T(8,128)S(1)}, u32[]{:S(2)}, u32[]{:S(2)}) %collective-permute-start.2) | collective-permute-done | bytes 262176 | tf_op jit(solution)/shard_map/ppermute | solution.py:38
  45.2 5.6 %collective-permute-start.4 = (f32[64,1024]{1,0:T(8,128)S(1)}, f32[64,1024]{1,0:T(8,128)S(1)}, u32[]{:S(2)}, u32[]{:S(2)}) collective-permute-start(f32[64,1024]{1,0:T(8,128)S(1)} %collective-permute-done.2), channel_id=1, source_target_pairs={{0,224},{1,33},{32,0},{33,65},{64,32},{65,97},{96,64},{97,129},{12... | collective-permute-start | bytes 786440 | tf_op jit(solution)/shard_map/ppermute | solution.py:38
  50.8 1.7 %collective-permute-done.3 = f32[64,1024]{1,0:T(8,128)S(1)} collective-permute-done((f32[64,1024]{1,0:T(8,128)S(1)}, f32[64,1024]{1,0:T(8,128)S(1)}, u32[]{:S(2)}, u32[]{:S(2)}) %collective-permute-start.3) | collective-permute-done | bytes 262176 | tf_op jit(solution)/shard_map/ppermute | solution.py:38
  52.5 1.9 %collective-permute-start.5 = (f32[64,1024]{1,0:T(8,128)S(1)}, f32[64,1024]{1,0:T(8,128)S(1)}, u32[]{:S(2)}, u32[]{:S(2)}) collective-permute-start(f32[64,1024]{1,0:T(8,128)S(1)} %collective-permute-done.3), channel_id=1, source_target_pairs={{0,32},{1,225},{32,64},{33,1},{64,96},{65,33},{96,128},{97,65},{12... | collective-permute-start | bytes 786440 | tf_op jit(solution)/shard_map/ppermute | solution.py:38
  54.8 5.6 %collective-permute-start.6 = (f32[64,1024]{1,0:T(8,128)S(1)}, f32[64,1024]{1,0:T(8,128)S(1)}, u32[]{:S(2)}, u32[]{:S(2)}) collective-permute-start(f32[64,1024]{1,0:T(8,128)S(1)} %collective-permute-done.4), channel_id=1, source_target_pairs={{0,224},{1,33},{32,0},{33,65},{64,32},{65,97},{96,64},{97,129},{12... | collective-permute-start | bytes 786440 | tf_op jit(solution)/shard_map/ppermute | solution.py:38
  60.4 3.5 %collective-permute-done.5 = f32[64,1024]{1,0:T(8,128)S(1)} collective-permute-done((f32[64,1024]{1,0:T(8,128)S(1)}, f32[64,1024]{1,0:T(8,128)S(1)}, u32[]{:S(2)}, u32[]{:S(2)}) %collective-permute-start.5) | collective-permute-done | bytes 262176 | tf_op jit(solution)/shard_map/ppermute | solution.py:38
  64.3 1.3 %copy-done = f32[8,64,1024]{2,1,0:T(8,128)} copy-done((f32[8,64,1024]{2,1,0:T(8,128)}, f32[8,64,1024]{2,1,0:T(8,128)S(1)}, u32[]{:S(2)}) %copy-start) | copy-done | bytes 2097176
  65.6 1.6 %copy-done.1 = f32[8,64,1024]{2,1,0:T(8,128)S(1)} copy-done((f32[8,64,1024]{2,1,0:T(8,128)S(1)}, f32[8,64,1024]{2,1,0:T(8,128)}, u32[]{:S(2)}) %copy-start.1) | copy-done | bytes 2097176
  67.2 1.7 %shard_map.29 = (f32[32,9,4,128]{3,2,1,0:T(4,128)S(1)}, f32[4,128]{1,0:T(4,128)S(1)}) custom-call(s32[1]{0:T(128)} %bitcast.16.core_ref, f32[8,256,256]{2,1,0:T(8,128)S(1)} %all-to-all-done.left_ref, f32[512,1024]{1,0:T(8,128)S(1)} %bitcast.26), custom_call_target="tpu_custom_call" | custom-call | flops 805306368 | bytes 4784128 | tf_op jit(solution)/shard_map/pallas_call | solution.py:122
  68.9 1.9 %collective-permute-start.7 = (f32[32,9,4,128]{3,2,1,0:T(4,128)S(1)}, f32[32,9,4,128]{3,2,1,0:T(4,128)S(1)}, u32[]{:S(2)}, u32[]{:S(2)}) collective-permute-start(f32[32,9,4,128]{3,2,1,0:T(4,128)S(1)} %get-tuple-element.12), channel_id=1, source_target_pairs={{0,1},{1,0},{32,33},{33,32},{64,65},{65,64},{96,97},{97,96},{128,1... | collective-permute-start | bytes 1769480 | tf_op jit(solution)/shard_map/ppermute | solution.py:38
  70.9 1.1 %shard_map.30 = f32[32,9,4,128]{3,2,1,0:T(4,128)S(1)} custom-call(s32[1]{0:T(128)} %bitcast.4.core_ref, f32[8,256,256]{2,1,0:T(8,128)S(1)} %all-to-all-done.left_ref, f32[512,1024]{1,0:T(8,128)S(1)} %bitcast.27, f32[4,128]{1,0:T(4,128)S(1)} %get-tuple-element.11.refs_0_), custom_call_target="tpu_custom_call" | custom-call | flops 805306368 | bytes 4784128 | tf_op jit(solution)/shard_map/pallas_call | solution.py:122
  72.8 1.0 add.99
  73.8 10.2 %all-to-all-start.2 = ((f32[32,9,4,128]{3,2,1,0:T(4,128)}), f32[32,9,4,128]{3,2,1,0:T(4,128)S(1)}, u32[]{:S(2)}, u32[]{:S(2)}) async-start(f32[32,9,4,128]{3,2,1,0:T(4,128)} %add.99), calls=%async_computation.2 | async-start | bytes 1179648 | tf_op jit(solution)/shard_map/all_to_all | solution.py:188
  84.2 19.1 %all-to-all-done.2.whole_ref = f32[32,9,4,128]{3,2,1,0:T(4,128)S(1)} async-done(((f32[32,9,4,128]{3,2,1,0:T(4,128)}), f32[32,9,4,128]{3,2,1,0:T(4,128)S(1)}, u32[]{:S(2)}, u32[]{:S(2)}) %all-to-all-start.2) | async-done | bytes 589856 | tf_op jit(solution)/shard_map/all_to_all | solution.py:188
  103.3 1.4 %shard_map.31 = f32[8,4096]{1,0:T(8,128)} custom-call(s32[4]{0:T(128)S(1)} %pad_add_fusion.place_ref, f32[32,9,4,128]{3,2,1,0:T(4,128)S(1)} %all-to-all-done.2.whole_ref), custom_call_target="tpu_custom_call" | custom-call | flops 262144 | bytes 786432 | tf_op jit(solution)/shard_map/pallas_call | solution.py:163
  (25 shorter events, 3.2 us)
Async XLA Ops:
  0.0 0.9 copy-start.3
  1.0 0.7 copy-start.4
  1.8 1.3 %copy-start.2 = (f32[8,256,256]{2,1,0:T(8,128)}, f32[8,256,256]{2,1,0:T(8,128)S(1)}, u32[]{:S(2)}) copy-start(f32[8,256,256]{2,1,0:T(8,128)S(1)} %get-tuple-element.9) | copy-start | bytes 6291460
  13.9 51.7 %all-to-all-start = ((f32[8,256,256]{2,1,0:T(8,128)}), f32[8,256,256]{2,1,0:T(8,128)S(1)}, u32[]{:S(2)}, u32[]{:S(2)}) async-start(f32[8,256,256]{2,1,0:T(8,128)} %copy-done.2), calls=%async_computation | async-start | bytes 4194304 | tf_op jit(solution)/shard_map/all_to_all | solution.py:182
  21.5 13.1 %collective-permute-start = (f32[64,1024]{1,0:T(8,128)S(1)}, f32[64,1024]{1,0:T(8,128)S(1)}, u32[]{:S(2)}, u32[]{:S(2)}) collective-permute-start(f32[64,1024]{1,0:T(8,128)S(1)} %bitcast.32), channel_id=1, source_target_pairs={{0,224},{1,33},{32,0},{33,65},{64,32},{65,97},{96,64},{97,129},{12... | collective-permute-start | bytes 786440 | tf_op jit(solution)/shard_map/ppermute | solution.py:38
  28.8 11.4 %collective-permute-start.1 = (f32[64,1024]{1,0:T(8,128)S(1)}, f32[64,1024]{1,0:T(8,128)S(1)}, u32[]{:S(2)}, u32[]{:S(2)}) collective-permute-start(f32[64,1024]{1,0:T(8,128)S(1)} %bitcast.33), channel_id=1, source_target_pairs={{0,32},{1,225},{32,64},{33,1},{64,96},{65,33},{96,128},{97,65},{12... | collective-permute-start | bytes 786440 | tf_op jit(solution)/shard_map/ppermute | solution.py:38
  34.6 10.5 %collective-permute-start.2 = (f32[64,1024]{1,0:T(8,128)S(1)}, f32[64,1024]{1,0:T(8,128)S(1)}, u32[]{:S(2)}, u32[]{:S(2)}) collective-permute-start(f32[64,1024]{1,0:T(8,128)S(1)} %collective-permute-done), channel_id=1, source_target_pairs={{0,224},{1,33},{32,0},{33,65},{64,32},{65,97},{96,64},{97,129},{12... | collective-permute-start | bytes 786440 | tf_op jit(solution)/shard_map/ppermute | solution.py:38
  40.2 12.3 %collective-permute-start.3 = (f32[64,1024]{1,0:T(8,128)S(1)}, f32[64,1024]{1,0:T(8,128)S(1)}, u32[]{:S(2)}, u32[]{:S(2)}) collective-permute-start(f32[64,1024]{1,0:T(8,128)S(1)} %collective-permute-done.1), channel_id=1, source_target_pairs={{0,32},{1,225},{32,64},{33,1},{64,96},{65,33},{96,128},{97,65},{12... | collective-permute-start | bytes 786440 | tf_op jit(solution)/shard_map/ppermute | solution.py:38
  45.2 9.6 %collective-permute-start.4 = (f32[64,1024]{1,0:T(8,128)S(1)}, f32[64,1024]{1,0:T(8,128)S(1)}, u32[]{:S(2)}, u32[]{:S(2)}) collective-permute-start(f32[64,1024]{1,0:T(8,128)S(1)} %collective-permute-done.2), channel_id=1, source_target_pairs={{0,224},{1,33},{32,0},{33,65},{64,32},{65,97},{96,64},{97,129},{12... | collective-permute-start | bytes 786440 | tf_op jit(solution)/shard_map/ppermute | solution.py:38
  52.5 11.4 %collective-permute-start.5 = (f32[64,1024]{1,0:T(8,128)S(1)}, f32[64,1024]{1,0:T(8,128)S(1)}, u32[]{:S(2)}, u32[]{:S(2)}) collective-permute-start(f32[64,1024]{1,0:T(8,128)S(1)} %collective-permute-done.3), channel_id=1, source_target_pairs={{0,32},{1,225},{32,64},{33,1},{64,96},{65,33},{96,128},{97,65},{12... | collective-permute-start | bytes 786440 | tf_op jit(solution)/shard_map/ppermute | solution.py:38
  54.8 9.5 %collective-permute-start.6 = (f32[64,1024]{1,0:T(8,128)S(1)}, f32[64,1024]{1,0:T(8,128)S(1)}, u32[]{:S(2)}, u32[]{:S(2)}) collective-permute-start(f32[64,1024]{1,0:T(8,128)S(1)} %collective-permute-done.4), channel_id=1, source_target_pairs={{0,224},{1,33},{32,0},{33,65},{64,32},{65,97},{96,64},{97,129},{12... | collective-permute-start | bytes 786440 | tf_op jit(solution)/shard_map/ppermute | solution.py:38
  64.3 1.3 %copy-start = (f32[8,64,1024]{2,1,0:T(8,128)}, f32[8,64,1024]{2,1,0:T(8,128)S(1)}, u32[]{:S(2)}) copy-start(f32[8,64,1024]{2,1,0:T(8,128)S(1)} %bitcast_dynamic-update-slice_fusion) | copy-start | bytes 6291460
  65.6 1.6 %copy-start.1 = (f32[8,64,1024]{2,1,0:T(8,128)S(1)}, f32[8,64,1024]{2,1,0:T(8,128)}, u32[]{:S(2)}) copy-start(f32[8,64,1024]{2,1,0:T(8,128)} %copy-done) | copy-start | bytes 6291460
  68.9 3.9 %collective-permute-start.7 = (f32[32,9,4,128]{3,2,1,0:T(4,128)S(1)}, f32[32,9,4,128]{3,2,1,0:T(4,128)S(1)}, u32[]{:S(2)}, u32[]{:S(2)}) collective-permute-start(f32[32,9,4,128]{3,2,1,0:T(4,128)S(1)} %get-tuple-element.12), channel_id=1, source_target_pairs={{0,1},{1,0},{32,33},{33,32},{64,65},{65,64},{96,97},{97,96},{128,1... | collective-permute-start | bytes 1769480 | tf_op jit(solution)/shard_map/ppermute | solution.py:38
  73.8 29.5 %all-to-all-start.2 = ((f32[32,9,4,128]{3,2,1,0:T(4,128)}), f32[32,9,4,128]{3,2,1,0:T(4,128)S(1)}, u32[]{:S(2)}, u32[]{:S(2)}) async-start(f32[32,9,4,128]{3,2,1,0:T(4,128)} %add.99), calls=%async_computation.2 | async-start | bytes 1179648 | tf_op jit(solution)/shard_map/all_to_all | solution.py:188

commit v7 on v6

--- a/solution.py
+++ b/solution.py
@@ -79,7 +79,7 @@
 
 
 def half_kernel(first, core_ref, left_ref, right_ref, *refs):
-    message_ref, tile_ref, total_ref = (refs[0], refs[1], refs[2]) if first else (refs[1], refs[0], refs[2])
+    message_ref, tile_ref, total_ref = (refs[0], refs[1], refs[3]) if first else (refs[1], refs[0], refs[2])
     core = core_ref[0]
     ones = jnp.ones((8, 256), jnp.bfloat16)
     sums = jnp.zeros((8, 512), jnp.float32)
@@ -119,11 +119,13 @@
     first = tile is None
     message = jax.ShapeDtypeStruct((XS * YS, 9, 4, 128), jnp.float32)
     sums = jax.ShapeDtypeStruct((4, 128), jnp.float32)
+    same = jax.ShapeDtypeStruct(right.shape, jnp.float32)
     return pl.pallas_call(
         functools.partial(half_kernel, first),
-        out_shape=(message, sums) if first else message,
+        out_shape=(message, sums, same) if first else message,
         in_specs=[SMEM] + [VMEM] * (2 if first else 3),
-        out_specs=(VMEM, VMEM) if first else VMEM,
+        out_specs=(VMEM, VMEM, VMEM) if first else VMEM,
+        input_output_aliases={2: 2} if first else {},
         scratch_shapes=[pltpu.VMEM((256, 512), jnp.float32)],
         compiler_params=PARAMS,
         cost_estimate=pl.CostEstimate(flops=3 * 2 * 256 * 512 * 1024, bytes_accessed=4784128, transcendentals=0),
@@ -182,7 +184,7 @@
     left = lax.all_to_all(copies, AXES, 0, 0, axis_index_groups=LEFT_GROUPS, tiled=True)
     right = ring(piece, z, 1 - 2 * core)
 
-    theirs, tile = half_product(1 - core, left, right)
+    theirs, tile, right = half_product(1 - core, left, right)
     theirs = shift(theirs, lambda x, y, z, c: (x, y, z, c + 1))
     mine = half_product(core, left, right, tile) + theirs
     whole = lax.all_to_all(mine, AXES, 0, 0, axis_index_groups=XY_GROUPS, tiled=True)

time: 105 us -> 105 us (level)
  no operation moved by 1% of the time
where the time goes in v7:
time: 105 us
  starting transfers between devices  49.6 us (47%)
  waiting for transfers between devices  31.9 us (30%)
  blocking collectives  10.8 us (10%)
  local copies, waits for them, and re-layouts  6.62 us (6%)
  Pallas kernels  4.39 us (4%)
  other arithmetic  1.06 us (1%)
    ppermute x8, starting transfers between devices, shift(): return lax.ppermute(value, AXES, pairs)  31.7 us
    all_to_all x1, waiting for transfers between devices, shards(): lax.all_to_all(mine, AXES, 0, 0, axis_index_groups=XY_GROUPS, tiled=True)  19.1 us
    ppermute x8, waiting for transfers between devices, shift(): return lax.ppermute(value, AXES, pairs)  12.7 us
    all_to_all x1, blocking collectives, shards(): lax.all_to_all(scaled.reshape(XS, 64, 256), 'feat', 0, 0, axis_index_grou...  10.8 us
    all_to_all x1, starting transfers between devices, shards(): lax.all_to_all(mine, AXES, 0, 0, axis_index_groups=XY_GROUPS, tiled=True)  10.2 us
    all_to_all x1, starting transfers between devices, shards(): lax.all_to_all(copies, AXES, 0, 0, axis_index_groups=LEFT_GROUPS, tiled=T...  7.62 us
    unnamed x10, local copies, waits for them, and re-layouts  5.86 us
    pallas_call x2, Pallas kernels, half_product(): pl.pallas_call(functools.partial(half_kernel, first), out_shape=(message,...  2.82 us
  transfers between devices with their start and end apart: 10, of which 8 were waited for; matrix products, arithmetic and copies ran while one was open for 1% of the time, Pallas kernels for 1%

profile of v7, /device:TPU:8, one launch (start us, length us, event | category | flops | bytes accessed | tf_op | source)
XLA Modules:
  0.0 104.7 jit_solution(15291116162128451967)
XLA Ops:
  0.0 0.9 copy-done.3
  1.8 1.3 %copy-done.2 = f32[8,256,256]{2,1,0:T(8,128)} copy-done((f32[8,256,256]{2,1,0:T(8,128)}, f32[8,256,256]{2,1,0:T(8,128)S(1)}, u32[]{:S(2)}) %copy-start.2) | copy-done | bytes 2097176
  3.1 10.8 %all_to_all.15 = f32[4,64,256]{2,1,0:T(8,128)S(1)} all-to-all(f32[4,64,256]{2,1,0:T(8,128)S(1)} %bitcast.27), channel_id=1, replica_groups={{0,8,16,24},{1,9,17,25},{2,10,18,26},{3,11,19,27},{4,12,20,28},{5,13,21..., dimensions={0} | all-to-all | bytes 524288 | tf_op jit(solution)/shard_map/all_to_all | solution.py:182
  13.9 7.6 %all-to-all-start = ((f32[8,256,256]{2,1,0:T(8,128)}), f32[8,256,256]{2,1,0:T(8,128)S(1)}, u32[]{:S(2)}, u32[]{:S(2)}) async-start(f32[8,256,256]{2,1,0:T(8,128)} %copy-done.2), calls=%async_computation | async-start | bytes 4194304 | tf_op jit(solution)/shard_map/all_to_all | solution.py:184
  21.5 7.3 %collective-permute-start = (f32[64,1024]{1,0:T(8,128)S(1)}, f32[64,1024]{1,0:T(8,128)S(1)}, u32[]{:S(2)}, u32[]{:S(2)}) collective-permute-start(f32[64,1024]{1,0:T(8,128)S(1)} %bitcast.31), channel_id=1, source_target_pairs={{0,224},{1,33},{32,0},{33,65},{64,32},{65,97},{96,64},{97,129},{12... | collective-permute-start | bytes 786440 | tf_op jit(solution)/shard_map/ppermute | solution.py:38
  28.8 1.9 %collective-permute-start.1 = (f32[64,1024]{1,0:T(8,128)S(1)}, f32[64,1024]{1,0:T(8,128)S(1)}, u32[]{:S(2)}, u32[]{:S(2)}) collective-permute-start(f32[64,1024]{1,0:T(8,128)S(1)} %bitcast.32), channel_id=1, source_target_pairs={{0,32},{1,225},{32,64},{33,1},{64,96},{65,33},{96,128},{97,65},{12... | collective-permute-start | bytes 786440 | tf_op jit(solution)/shard_map/ppermute | solution.py:38
  31.5 3.1 %collective-permute-done = f32[64,1024]{1,0:T(8,128)S(1)} collective-permute-done((f32[64,1024]{1,0:T(8,128)S(1)}, f32[64,1024]{1,0:T(8,128)S(1)}, u32[]{:S(2)}, u32[]{:S(2)}) %collective-permute-start) | collective-permute-done | bytes 262176 | tf_op jit(solution)/shard_map/ppermute | solution.py:38
  34.6 5.6 %collective-permute-start.2 = (f32[64,1024]{1,0:T(8,128)S(1)}, f32[64,1024]{1,0:T(8,128)S(1)}, u32[]{:S(2)}, u32[]{:S(2)}) collective-permute-start(f32[64,1024]{1,0:T(8,128)S(1)} %collective-permute-done), channel_id=1, source_target_pairs={{0,224},{1,33},{32,0},{33,65},{64,32},{65,97},{96,64},{97,129},{12... | collective-permute-start | bytes 786440 | tf_op jit(solution)/shard_map/ppermute | solution.py:38
  40.2 1.9 %collective-permute-start.3 = (f32[64,1024]{1,0:T(8,128)S(1)}, f32[64,1024]{1,0:T(8,128)S(1)}, u32[]{:S(2)}, u32[]{:S(2)}) collective-permute-start(f32[64,1024]{1,0:T(8,128)S(1)} %collective-permute-done.1), channel_id=1, source_target_pairs={{0,32},{1,225},{32,64},{33,1},{64,96},{65,33},{96,128},{97,65},{12... | collective-permute-start | bytes 786440 | tf_op jit(solution)/shard_map/ppermute | solution.py:38
  42.2 2.9 %collective-permute-done.2 = f32[64,1024]{1,0:T(8,128)S(1)} collective-permute-done((f32[64,1024]{1,0:T(8,128)S(1)}, f32[64,1024]{1,0:T(8,128)S(1)}, u32[]{:S(2)}, u32[]{:S(2)}) %collective-permute-start.2) | collective-permute-done | bytes 262176 | tf_op jit(solution)/shard_map/ppermute | solution.py:38
  45.2 5.6 %collective-permute-start.4 = (f32[64,1024]{1,0:T(8,128)S(1)}, f32[64,1024]{1,0:T(8,128)S(1)}, u32[]{:S(2)}, u32[]{:S(2)}) collective-permute-start(f32[64,1024]{1,0:T(8,128)S(1)} %collective-permute-done.2), channel_id=1, source_target_pairs={{0,224},{1,33},{32,0},{33,65},{64,32},{65,97},{96,64},{97,129},{12... | collective-permute-start | bytes 786440 | tf_op jit(solution)/shard_map/ppermute | solution.py:38
  50.8 1.7 %collective-permute-done.3 = f32[64,1024]{1,0:T(8,128)S(1)} collective-permute-done((f32[64,1024]{1,0:T(8,128)S(1)}, f32[64,1024]{1,0:T(8,128)S(1)}, u32[]{:S(2)}, u32[]{:S(2)}) %collective-permute-start.3) | collective-permute-done | bytes 262176 | tf_op jit(solution)/shard_map/ppermute | solution.py:38
  52.5 1.9 %collective-permute-start.5 = (f32[64,1024]{1,0:T(8,128)S(1)}, f32[64,1024]{1,0:T(8,128)S(1)}, u32[]{:S(2)}, u32[]{:S(2)}) collective-permute-start(f32[64,1024]{1,0:T(8,128)S(1)} %collective-permute-done.3), channel_id=1, source_target_pairs={{0,32},{1,225},{32,64},{33,1},{64,96},{65,33},{96,128},{97,65},{12... | collective-permute-start | bytes 786440 | tf_op jit(solution)/shard_map/ppermute | solution.py:38
  54.8 5.6 %collective-permute-start.6 = (f32[64,1024]{1,0:T(8,128)S(1)}, f32[64,1024]{1,0:T(8,128)S(1)}, u32[]{:S(2)}, u32[]{:S(2)}) collective-permute-start(f32[64,1024]{1,0:T(8,128)S(1)} %collective-permute-done.4), channel_id=1, source_target_pairs={{0,224},{1,33},{32,0},{33,65},{64,32},{65,97},{96,64},{97,129},{12... | collective-permute-start | bytes 786440 | tf_op jit(solution)/shard_map/ppermute | solution.py:38
  60.4 3.5 %collective-permute-done.5 = f32[64,1024]{1,0:T(8,128)S(1)} collective-permute-done((f32[64,1024]{1,0:T(8,128)S(1)}, f32[64,1024]{1,0:T(8,128)S(1)}, u32[]{:S(2)}, u32[]{:S(2)}) %collective-permute-start.5) | collective-permute-done | bytes 262176 | tf_op jit(solution)/shard_map/ppermute | solution.py:38
  64.3 1.3 %copy-done = f32[8,64,1024]{2,1,0:T(8,128)} copy-done((f32[8,64,1024]{2,1,0:T(8,128)}, f32[8,64,1024]{2,1,0:T(8,128)S(1)}, u32[]{:S(2)}) %copy-start) | copy-done | bytes 2097176
  65.6 1.6 %copy-done.1 = f32[8,64,1024]{2,1,0:T(8,128)S(1)} copy-done((f32[8,64,1024]{2,1,0:T(8,128)S(1)}, f32[8,64,1024]{2,1,0:T(8,128)}, u32[]{:S(2)}) %copy-start.1) | copy-done | bytes 2097176
  67.2 1.7 %shard_map.29 = (f32[32,9,4,128]{3,2,1,0:T(4,128)S(1)}, f32[4,128]{1,0:T(4,128)S(1)}, f32[512,1024]{1,0:T(8,128)S(1)}) custom-call(s32[1]{0:T(128)} %bitcast.6.core_ref, f32[8,256,256]{2,1,0:T(8,128)S(1)} %all-to-all-done.left_ref, f32[512,1024]{1,0:T(8,128)S(1)} %bitcast.26), custom_call_target="tpu_custom_call", output_to_operand_aliasing={{2}: (2, {})} | custom-call | flops 805306368 | bytes 4784128 | tf_op jit(solution)/shard_map/pallas_call | solution.py:123
  68.9 1.9 %collective-permute-start.7 = (f32[32,9,4,128]{3,2,1,0:T(4,128)S(1)}, f32[32,9,4,128]{3,2,1,0:T(4,128)S(1)}, u32[]{:S(2)}, u32[]{:S(2)}) collective-permute-start(f32[32,9,4,128]{3,2,1,0:T(4,128)S(1)} %get-tuple-element.14), channel_id=1, source_target_pairs={{0,1},{1,0},{32,33},{33,32},{64,65},{65,64},{96,97},{97,96},{128,1... | collective-permute-start | bytes 1769480 | tf_op jit(solution)/shard_map/ppermute | solution.py:38
  70.9 1.1 %shard_map.30 = f32[32,9,4,128]{3,2,1,0:T(4,128)S(1)} custom-call(s32[1]{0:T(128)} %bitcast.4.core_ref, f32[8,256,256]{2,1,0:T(8,128)S(1)} %all-to-all-done.left_ref, f32[512,1024]{1,0:T(8,128)S(1)} %get-tuple-element.12.right_ref, f32[4,128]{1,0:T(4,128)S(1)} %get-tuple-element.13.refs_0_), custom_call_target="tpu_custom_call" | custom-call | flops 805306368 | bytes 4784128 | tf_op jit(solution)/shard_map/pallas_call | solution.py:123
  72.8 1.0 add.99
  73.8 10.2 %all-to-all-start.2 = ((f32[32,9,4,128]{3,2,1,0:T(4,128)}), f32[32,9,4,128]{3,2,1,0:T(4,128)S(1)}, u32[]{:S(2)}, u32[]{:S(2)}) async-start(f32[32,9,4,128]{3,2,1,0:T(4,128)} %add.99), calls=%async_computation.2 | async-start | bytes 1179648 | tf_op jit(solution)/shard_map/all_to_all | solution.py:190
  84.2 19.1 %all-to-all-done.2.whole_ref = f32[32,9,4,128]{3,2,1,0:T(4,128)S(1)} async-done(((f32[32,9,4,128]{3,2,1,0:T(4,128)}), f32[32,9,4,128]{3,2,1,0:T(4,128)S(1)}, u32[]{:S(2)}, u32[]{:S(2)}) %all-to-all-start.2) | async-done | bytes 589856 | tf_op jit(solution)/shard_map/all_to_all | solution.py:190
  103.3 1.4 %shard_map.31 = f32[8,4096]{1,0:T(8,128)} custom-call(s32[4]{0:T(128)S(1)} %pad_add_fusion.place_ref, f32[32,9,4,128]{3,2,1,0:T(4,128)S(1)} %all-to-all-done.2.whole_ref), custom_call_target="tpu_custom_call" | custom-call | flops 262144 | bytes 786432 | tf_op jit(solution)/shard_map/pallas_call | solution.py:165
  (25 shorter events, 3.2 us)
Async XLA Ops:
  0.0 0.9 copy-start.3
  1.0 0.7 copy-start.4
  1.8 1.3 %copy-start.2 = (f32[8,256,256]{2,1,0:T(8,128)}, f32[8,256,256]{2,1,0:T(8,128)S(1)}, u32[]{:S(2)}) copy-start(f32[8,256,256]{2,1,0:T(8,128)S(1)} %get-tuple-element.10) | copy-start | bytes 6291460
  13.9 51.7 %all-to-all-start = ((f32[8,256,256]{2,1,0:T(8,128)}), f32[8,256,256]{2,1,0:T(8,128)S(1)}, u32[]{:S(2)}, u32[]{:S(2)}) async-start(f32[8,256,256]{2,1,0:T(8,128)} %copy-done.2), calls=%async_computation | async-start | bytes 4194304 | tf_op jit(solution)/shard_map/all_to_all | solution.py:184
  21.5 13.1 %collective-permute-start = (f32[64,1024]{1,0:T(8,128)S(1)}, f32[64,1024]{1,0:T(8,128)S(1)}, u32[]{:S(2)}, u32[]{:S(2)}) collective-permute-start(f32[64,1024]{1,0:T(8,128)S(1)} %bitcast.31), channel_id=1, source_target_pairs={{0,224},{1,33},{32,0},{33,65},{64,32},{65,97},{96,64},{97,129},{12... | collective-permute-start | bytes 786440 | tf_op jit(solution)/shard_map/ppermute | solution.py:38
  28.8 11.4 %collective-permute-start.1 = (f32[64,1024]{1,0:T(8,128)S(1)}, f32[64,1024]{1,0:T(8,128)S(1)}, u32[]{:S(2)}, u32[]{:S(2)}) collective-permute-start(f32[64,1024]{1,0:T(8,128)S(1)} %bitcast.32), channel_id=1, source_target_pairs={{0,32},{1,225},{32,64},{33,1},{64,96},{65,33},{96,128},{97,65},{12... | collective-permute-start | bytes 786440 | tf_op jit(solution)/shard_map/ppermute | solution.py:38
  34.6 10.5 %collective-permute-start.2 = (f32[64,1024]{1,0:T(8,128)S(1)}, f32[64,1024]{1,0:T(8,128)S(1)}, u32[]{:S(2)}, u32[]{:S(2)}) collective-permute-start(f32[64,1024]{1,0:T(8,128)S(1)} %collective-permute-done), channel_id=1, source_target_pairs={{0,224},{1,33},{32,0},{33,65},{64,32},{65,97},{96,64},{97,129},{12... | collective-permute-start | bytes 786440 | tf_op jit(solution)/shard_map/ppermute | solution.py:38
  40.2 12.3 %collective-permute-start.3 = (f32[64,1024]{1,0:T(8,128)S(1)}, f32[64,1024]{1,0:T(8,128)S(1)}, u32[]{:S(2)}, u32[]{:S(2)}) collective-permute-start(f32[64,1024]{1,0:T(8,128)S(1)} %collective-permute-done.1), channel_id=1, source_target_pairs={{0,32},{1,225},{32,64},{33,1},{64,96},{65,33},{96,128},{97,65},{12... | collective-permute-start | bytes 786440 | tf_op jit(solution)/shard_map/ppermute | solution.py:38
  45.2 9.6 %collective-permute-start.4 = (f32[64,1024]{1,0:T(8,128)S(1)}, f32[64,1024]{1,0:T(8,128)S(1)}, u32[]{:S(2)}, u32[]{:S(2)}) collective-permute-start(f32[64,1024]{1,0:T(8,128)S(1)} %collective-permute-done.2), channel_id=1, source_target_pairs={{0,224},{1,33},{32,0},{33,65},{64,32},{65,97},{96,64},{97,129},{12... | collective-permute-start | bytes 786440 | tf_op jit(solution)/shard_map/ppermute | solution.py:38
  52.5 11.4 %collective-permute-start.5 = (f32[64,1024]{1,0:T(8,128)S(1)}, f32[64,1024]{1,0:T(8,128)S(1)}, u32[]{:S(2)}, u32[]{:S(2)}) collective-permute-start(f32[64,1024]{1,0:T(8,128)S(1)} %collective-permute-done.3), channel_id=1, source_target_pairs={{0,32},{1,225},{32,64},{33,1},{64,96},{65,33},{96,128},{97,65},{12... | collective-permute-start | bytes 786440 | tf_op jit(solution)/shard_map/ppermute | solution.py:38
  54.8 9.5 %collective-permute-start.6 = (f32[64,1024]{1,0:T(8,128)S(1)}, f32[64,1024]{1,0:T(8,128)S(1)}, u32[]{:S(2)}, u32[]{:S(2)}) collective-permute-start(f32[64,1024]{1,0:T(8,128)S(1)} %collective-permute-done.4), channel_id=1, source_target_pairs={{0,224},{1,33},{32,0},{33,65},{64,32},{65,97},{96,64},{97,129},{12... | collective-permute-start | bytes 786440 | tf_op jit(solution)/shard_map/ppermute | solution.py:38
  64.3 1.3 %copy-start = (f32[8,64,1024]{2,1,0:T(8,128)}, f32[8,64,1024]{2,1,0:T(8,128)S(1)}, u32[]{:S(2)}) copy-start(f32[8,64,1024]{2,1,0:T(8,128)S(1)} %bitcast_dynamic-update-slice_fusion) | copy-start | bytes 6291460
  65.6 1.6 %copy-start.1 = (f32[8,64,1024]{2,1,0:T(8,128)S(1)}, f32[8,64,1024]{2,1,0:T(8,128)}, u32[]{:S(2)}) copy-start(f32[8,64,1024]{2,1,0:T(8,128)} %copy-done) | copy-start | bytes 6291460
  68.9 3.9 %collective-permute-start.7 = (f32[32,9,4,128]{3,2,1,0:T(4,128)S(1)}, f32[32,9,4,128]{3,2,1,0:T(4,128)S(1)}, u32[]{:S(2)}, u32[]{:S(2)}) collective-permute-start(f32[32,9,4,128]{3,2,1,0:T(4,128)S(1)} %get-tuple-element.14), channel_id=1, source_target_pairs={{0,1},{1,0},{32,33},{33,32},{64,65},{65,64},{96,97},{97,96},{128,1... | collective-permute-start | bytes 1769480 | tf_op jit(solution)/shard_map/ppermute | solution.py:38
  73.8 29.5 %all-to-all-start.2 = ((f32[32,9,4,128]{3,2,1,0:T(4,128)}), f32[32,9,4,128]{3,2,1,0:T(4,128)S(1)}, u32[]{:S(2)}, u32[]{:S(2)}) async-start(f32[32,9,4,128]{3,2,1,0:T(4,128)} %add.99), calls=%async_computation.2 | async-start | bytes 1179648 | tf_op jit(solution)/shard_map/all_to_all | solution.py:190
